TPU v7x, 512 devices: a whole 4x4x16 slice. The times are simulated.
512 devices in a mesh: grp: 4 (over y), cell: 128 (over z, x, core).
Axes of the slice: x: 4, y: 4, z: 16, core: 2. Of those that a mesh axis runs over, the one named last changes fastest.
Arguments:
- block_ids: int32 [16384, 64, 1], P(('grp', 'cell')), may hold values from 0 to 511; in each aligned block of 2048 rows (0 to 2047, 2048 to 4095, ..., all dimensions but the last counted through in order) at most 8 rows name the same one
- positions: float32 [3, 16384, 64], P(None, ('grp', 'cell')), may hold values from -1 to 1
- spacing: float32 [16384, 64], P(('grp', 'cell')), may hold values from 0.01 to 0.06
- lengths: int32 [16384], P(('grp', 'cell')), may hold values from 16 to 64
- color_grad: float32 [3, 16384], P(None, ('grp', 'cell')), may hold values from -6 to 6
- first_weight: bfloat16 [512, 96, 256], P('cell'), may hold values from -0.625 to 0.625
- first_bias: float32 [512, 256], P('cell'), may hold values from -3 to 3
- second_weight: bfloat16 [512, 256, 256], P('cell'), may hold values from -0.375 to 0.375
- second_bias: float32 [512, 256], P('cell'), may hold values from -3 to 3
- third_weight: bfloat16 [512, 4, 256], P('cell'), may hold values from -0.375 to 0.375
- third_bias: float32 [512, 4], P('cell'), may hold values from -4 to 4
Outputs:
- grad_first_weight: float32 [512, 96, 256], P('cell')
- grad_first_bias: float32 [512, 256], P('cell')
- grad_second_weight: float32 [512, 256, 256], P('cell')
- grad_second_bias: float32 [512, 256], P('cell')
- grad_third_weight: float32 [512, 4, 256], P('cell')
- grad_third_bias: float32 [512, 4], P('cell')
Inputs may be any that keep to these rules, and one draw needn't show every extreme that they name: `block_ids`: the 32 rays of one device hold at most 8 samples of any one block, and exactly 8 of some block on some device.
All inputs are finite; a program needn't handle non-finite values.
Results may differ from a plain program's by a relative error of at most 0.0095.
Values may be sent and summed in bfloat16 or wider, within the bound.
A program may use at most 64 MiB of HBM per device.

v0:
```python
import math

import jax
import jax.numpy as jnp
from jax import lax
from jax.sharding import PartitionSpec as P


def encode(points, levels):
    frequency = math.pi * jnp.exp2(jnp.arange(levels, dtype=jnp.float32) * (8.0 / levels))
    angles = (points[:, :, None] * frequency[None, None, :]).reshape(points.shape[0], 3 * levels)
    return jnp.concatenate([jnp.sin(angles), jnp.cos(angles)], axis=1).astype(jnp.bfloat16)


def swish_slope(pre):
    sigmo = jax.nn.sigmoid(pre)
    return sigmo * (1.0 + pre * (1.0 - sigmo))


def render(field_out, spacing, lengths):
    sample_index = jnp.arange(field_out.shape[1], dtype=jnp.int32)
    live_mask = sample_index[None, :] < lengths[:, None]
    density = jax.nn.softplus(field_out[:, :, 0])
    shade = jax.nn.sigmoid(field_out[:, :, 1:])
    depth_step = jnp.where(live_mask, density * spacing, 0.0)
    log_trans = depth_step - jnp.cumsum(depth_step, axis=1)
    weight = jnp.exp(log_trans) * -jnp.expm1(-depth_step)
    return jnp.sum(weight[:, :, None] * shade, axis=1).T


def table_product(onehot, values):
    if values.dtype == jnp.float32:
        return jnp.dot(
            onehot.astype(jnp.float32),
            values,
            precision=lax.Precision.HIGHEST,
            preferred_element_type=jnp.float32,
        )
    return jnp.dot(onehot.astype(values.dtype), values, preferred_element_type=jnp.float32).astype(
        values.dtype
    )


def spread_rows(values, slot_index, slot_total):
    step = math.gcd(slot_total, 512)

    def place_block(start):
        targets = start + jnp.arange(step, dtype=jnp.int32)
        onehot = targets[:, None] == slot_index[None, :]
        return table_product(onehot, values)

    starts = jnp.arange(slot_total // step, dtype=jnp.int32) * step
    return lax.map(place_block, starts).reshape(slot_total, values.shape[1])


def collect_rows(table, slot_index):
    total = slot_index.shape[0]
    step = math.gcd(total, 512)
    slot_range = jnp.arange(table.shape[0], dtype=jnp.int32)

    def fetch_block(indices):
        onehot = indices[:, None] == slot_range[None, :]
        return table_product(onehot, table)

    return lax.map(fetch_block, slot_index.reshape(total // step, step)).reshape(
        total, table.shape[1]
    )


def local(
    block_ids,
    positions,
    spacing,
    lengths,
    color_grad,
    first_weight,
    first_bias,
    second_weight,
    second_bias,
    third_weight,
    third_bias,
):
    cells = lax.axis_size("cell")
    local_blocks = first_weight.shape[0]
    levels = first_weight.shape[1] // 6
    channels = third_weight.shape[1]
    rays_here, samples = spacing.shape
    total = rays_here * samples
    block_count = local_blocks * cells
    capacity = max(2, 2 * total // block_count)
    slot_total = block_count * capacity
    flat_ids = block_ids.reshape(total)
    sorter = jnp.argsort(flat_ids, stable=True)
    sorted_ids = flat_ids[sorter]
    starts = jnp.searchsorted(sorted_ids, jnp.arange(block_count, dtype=jnp.int32), side="left")
    rank_in = jnp.arange(total, dtype=jnp.int32) - starts[sorted_ids]
    owner_of = sorted_ids // local_blocks
    local_of = sorted_ids % local_blocks
    slot_sorted = (local_of * cells + owner_of) * capacity + rank_in
    slot_index = jnp.zeros((total,), jnp.int32).at[sorter].set(slot_sorted)
    points = positions.reshape(3, total).T
    weights_all = (first_weight, first_bias, second_weight, second_bias, third_weight, third_bias)
    w_first, b_first, w_second, b_second, w_third, b_third = weights_all
    encoded = encode(points, levels)
    width = encoded.shape[1]
    send_buf = spread_rows(encoded, slot_index, slot_total)
    arrived = lax.all_to_all(
        send_buf.reshape(local_blocks, cells, capacity, width),
        "cell",
        split_axis=1,
        concat_axis=2,
        tiled=True,
    )
    features = arrived.reshape(local_blocks, slot_total // local_blocks, width)
    first_pre = (
        jnp.einsum("bnk,bkh->bnh", features, w_first, preferred_element_type=jnp.float32)
        + b_first[:, None, :]
    )
    first_act = jax.nn.silu(first_pre).astype(jnp.bfloat16)
    second_pre = (
        jnp.einsum("bnk,bkh->bnh", first_act, w_second, preferred_element_type=jnp.float32)
        + b_second[:, None, :]
    )
    second_act = jax.nn.silu(second_pre).astype(jnp.bfloat16)
    field_out = (
        jnp.einsum("bnh,bch->bnc", second_act, w_third, preferred_element_type=jnp.float32)
        + b_third[:, None, :]
    )
    returned = lax.all_to_all(
        field_out.reshape(local_blocks, 1, cells * capacity, channels),
        "cell",
        split_axis=2,
        concat_axis=1,
        tiled=True,
    )
    sample_out = collect_rows(returned.reshape(slot_total, channels), slot_index).reshape(
        rays_here, samples, channels
    )
    color, pullback = jax.vjp(lambda values: render(values, spacing, lengths), sample_out)
    out_grad = pullback(color_grad)[0].reshape(total, channels)
    grad_buf = spread_rows(out_grad, slot_index, slot_total)
    owner_grad = lax.all_to_all(
        grad_buf.reshape(local_blocks, cells, capacity, channels),
        "cell",
        split_axis=1,
        concat_axis=2,
        tiled=True,
    )
    owner_grad = owner_grad.reshape(local_blocks, slot_total // local_blocks, channels)
    highest = lax.Precision.HIGHEST
    second_grad = jnp.einsum(
        "bnc,bch->bnh", owner_grad, w_third.astype(jnp.float32), precision=highest
    )
    second_delta = (second_grad * swish_slope(second_pre)).astype(jnp.bfloat16)
    first_grad = jnp.einsum(
        "bnk,bhk->bnh", second_delta, w_second, preferred_element_type=jnp.float32
    )
    first_delta = (first_grad * swish_slope(first_pre)).astype(jnp.bfloat16)
    grad_first_weight = jnp.einsum(
        "bnk,bnh->bkh", features, first_delta, preferred_element_type=jnp.float32
    )
    grad_first_bias = jnp.sum(first_delta.astype(jnp.float32), axis=1)
    grad_second_weight = jnp.einsum(
        "bnk,bnh->bkh", first_act, second_delta, preferred_element_type=jnp.float32
    )
    grad_second_bias = jnp.sum(second_delta.astype(jnp.float32), axis=1)
    grad_third_weight = jnp.einsum(
        "bnc,bnh->bch", owner_grad, second_act.astype(jnp.float32), precision=highest
    )
    grad_third_bias = jnp.sum(owner_grad, axis=1)
    totals = lax.psum(
        (
            grad_first_weight,
            grad_first_bias,
            grad_second_weight,
            grad_second_bias,
            grad_third_weight,
            grad_third_bias,
        ),
        "grp",
    )
    return (totals[0], totals[1], totals[2], totals[3], totals[4], totals[5])


def solution(mesh):
    in_specs = (
        P(("grp", "cell"), None, None),
        P(None, ("grp", "cell"), None),
        P(("grp", "cell"), None),
        P(("grp", "cell")),
        P(None, ("grp", "cell")),
        P("cell", None, None),
        P("cell", None),
        P("cell", None, None),
        P("cell", None),
        P("cell", None, None),
        P("cell", None),
    )
    out_specs = (
        P("cell", None, None),
        P("cell", None),
        P("cell", None, None),
        P("cell", None),
        P("cell", None, None),
        P("cell", None),
    )
    return jax.shard_map(local, mesh=mesh, in_specs=in_specs, out_specs=out_specs, check_vma=False)
```

profile of v0, /device:TPU:1, one launch (start us, length us, event | category | flops | bytes accessed | tf_op | source)
XLA Modules:
  0.0 367.6 jit_solution(9471557155727576203)
XLA Ops:
  7.7 1.4 reduce.4
  9.2 5.0 %sort.17 = (s32[2048]{0:T(1024)}, s32[2048]{0:T(1024)S(1)}) sort(s32[2048]{0:T(1024)S(1)} %reshape.92, s32[2048]{0:T(1024)S(1)} %iota.39), dimensions={0}, to_apply=%region_0.0 | sort | flops 22528 | bytes 32768 | tf_op jit(solution)/shard_map/jit(argsort)/sort | solution.py:93
  14.3 11.8 %gather_fusion.1 = s32[2048]{0:T(1024)S(1)} fusion(s32[2048]{0:T(1024)S(1)} %reshape.92, s32[2048]{0:T(1024)S(1)} %get-tuple-element.260), kind=kCustom, calls=%fused_computation.1 | custom fusion | bytes 24576 | tf_op jit(solution)/shard_map/gather | solution.py:94
  26.1 38.9 %while.58 = (s32[]{:T(128)}, u32[512]{0:T(512)S(1)}, u32[512]{0:T(512)S(1)}, s32[2048]{0:T(1024)S(1)}, s32[]{:T(128)}, /*index=5*/s32[]{:T(128)}, s32[]{}) while((s32[]{:T(128)}, u32[512]{0:T(512)S(1)}, u32[512]{0:T(512)S(1)}, s32[2048]{0:T(1024)S(1)}, s32[]{:T(128)}, /*index=5*/s32[]{:T(128)}, s32[]{}) %tuple.93), condition=%wide.region_2.3_spmd.clone, body=%wide.region_1.2_spmd.clone.sunk | while | flops 10244 | bytes 37989 | solution.py:95
  26.1 3.1 gather_fusion
  29.4 3.1 gather_fusion
  32.6 3.1 gather_fusion
  35.9 3.1 gather_fusion
  39.1 3.1 gather_fusion
  42.3 3.1 gather_fusion
  45.6 3.1 gather_fusion
  48.8 3.1 gather_fusion
  52.0 3.1 gather_fusion
  55.3 3.1 gather_fusion
  58.5 3.1 gather_fusion
  61.8 3.1 gather_fusion
  65.0 13.2 %gather_fusion.2 = s32[2048]{0:T(1024)S(1)} fusion(s32[512]{0:T(512)S(1)} %convert_element_type.37, s32[2048]{0:T(1024)S(1)} %broadcast_clamp_fusion), kind=kCustom, calls=%fused_computation.2 | custom fusion | bytes 24576 | tf_op jit(solution)/shard_map/gather | solution.py:96
  78.4 1.6 fusion.36
  80.4 8.1 %scatter_custom_fusion = s32[2048]{0:T(1024)S(1)} fusion(s32[2048]{0:T(1024)S(1)} %get-tuple-element.261, s32[2048]{0:T(1024)S(1)} %fusion.51, s32[]{:T(128)} %constant.105.clone.1), kind=kCustom, calls=%fused_computation.93 | custom fusion | bytes 8196 | tf_op jit(solution)/shard_map/scatter | solution.py:100
  88.5 17.9 %while.55 = (s32[]{:T(128)}, bf16[8,512,96]{1,2,0:T(8,128)(2,1)S(1)}, s32[8]{0:T(128)S(1)}, s32[2048]{0:T(1024)S(1)}, bf16[2048,96]{1,0:T(8,128)(2,1)S(1)}, /*index=5*/s32[]{:T(128)}) while((s32[]{:T(128)}, bf16[8,512,96]{1,2,0:T(8,128)(2,1)S(1)}, s32[8]{0:T(128)S(1)}, s32[2048]{0:T(1024)S(1)}, bf16[2048,96]{1,0:T(8,128)(2,1)S(1)}, ...), condition=%wide.region_5.6_spmd, body=%wide.region_4.5_spmd.sunk | while | flops 202424832 | bytes 634969 | solution.py:53
  89.7 1.0 fusion.87
  91.9 1.0 fusion.87
  94.2 1.0 fusion.87
  96.4 1.0 fusion.87
  98.6 1.0 fusion.87
  100.9 1.0 fusion.87
  103.1 1.0 fusion.87
  105.3 1.0 fusion.87
  107.2 72.0 %all_to_all.12 = bf16[4,128,8,96]{3,2,0,1:T(8,128)(2,1)S(1)} all-to-all(bf16[4,128,8,96]{3,2,0,1:T(8,128)(2,1)S(1)} %copy.44), channel_id=1, replica_groups=mesh['grp'=4,'cell'=128] {'cell'}, dimensions={1} | all-to-all | bytes 1572864 | tf_op jit(solution)/shard_map/all_to_all | solution.py:107
  179.3 3.1 multiply_convert_fusion.3
  182.4 3.2 multiply_convert_fusion.2
  185.6 1.4 copy-done.1
  187.6 0.9 copy.47
  188.6 3.1 reshape.149
  191.7 10.2 %all-to-all-start.1 = ((f32[128,1,128]{2,1,0:T(1,128)}), f32[128,1,128]{2,1,0:T(1,128)S(1)}, u32[]{:S(2)}, u32[]{:S(2)}) async-start(f32[128,1,128]{2,1,0:T(1,128)} %reshape.149), calls=%async_computation.1 | async-start | bytes 131072 | tf_op jit(solution)/shard_map/all_to_all | solution.py:129
  202.2 14.5 %all-to-all-done.1 = f32[128,1,128]{2,1,0:T(1,128)S(1)} async-done(((f32[128,1,128]{2,1,0:T(1,128)}), f32[128,1,128]{2,1,0:T(1,128)S(1)}, u32[]{:S(2)}, u32[]{:S(2)}) %all-to-all-start.1) | async-done | bytes 65568 | tf_op jit(solution)/shard_map/all_to_all | solution.py:129
  218.0 2.7 reshape.150
  220.8 0.8 copy.48
  221.6 15.9 %while.57 = (s32[]{:T(128)}, f32[4,512,4]{1,0,2:T(4,128)S(1)}, s32[4,512]{1,0:T(4,128)S(1)}, f32[4096,4]{0,1:T(4,128)S(1)}, s32[]{:T(128)}, /*index=5*/s32[]{:T(128)}) while((s32[]{:T(128)}, f32[4,512,4]{1,0,2:T(4,128)S(1)}, s32[4,512]{1,0:T(4,128)S(1)}, f32[4096,4]{0,1:T(4,128)S(1)}, s32[]{:T(128)}, /*index=5*/s32[]{:T(128)}) %tuple.109), condition=%wide.region_7.8_spmd.clone, body=%wide.region_6.7_spmd.clone.sunk | while | flops 102760448 | bytes 112717 | solution.py:65
  221.6 3.9 %fusion.92 = f32[1,512,4]{1,2,0:T(4,128)S(1)} fusion(f32[4096,4]{0,1:T(4,128)S(1)} %get-tuple-element.440, s32[512]{0:T(512)S(1)} %bitcast.105), kind=kOutput, calls=%fused_computation.23.clone.1 | convolution fusion | flops 102760448 | bytes 75776 | tf_op jit(solution)/shard_map/while/body/eval_jaxpr/dot_general | solution.py:33
  225.6 3.9 %fusion.92 = f32[1,512,4]{1,2,0:T(4,128)S(1)} fusion(f32[4096,4]{0,1:T(4,128)S(1)} %get-tuple-element.440, s32[512]{0:T(512)S(1)} %bitcast.105), kind=kOutput, calls=%fused_computation.23.clone.1 | convolution fusion | flops 102760448 | bytes 75776 | tf_op jit(solution)/shard_map/while/body/eval_jaxpr/dot_general | solution.py:33
  229.6 3.9 %fusion.92 = f32[1,512,4]{1,2,0:T(4,128)S(1)} fusion(f32[4096,4]{0,1:T(4,128)S(1)} %get-tuple-element.440, s32[512]{0:T(512)S(1)} %bitcast.105), kind=kOutput, calls=%fused_computation.23.clone.1 | convolution fusion | flops 102760448 | bytes 75776 | tf_op jit(solution)/shard_map/while/body/eval_jaxpr/dot_general | solution.py:33
  233.6 3.9 %fusion.92 = f32[1,512,4]{1,2,0:T(4,128)S(1)} fusion(f32[4096,4]{0,1:T(4,128)S(1)} %get-tuple-element.440, s32[512]{0:T(512)S(1)} %bitcast.105), kind=kOutput, calls=%fused_computation.23.clone.1 | convolution fusion | flops 102760448 | bytes 75776 | tf_op jit(solution)/shard_map/while/body/eval_jaxpr/dot_general | solution.py:33
  238.7 26.0 %while.56 = (s32[]{:T(128)}, f32[8,512,4]{1,0,2:T(8,128)S(1)}, s32[8]{0:T(128)S(1)}, s32[2048]{0:T(1024)S(1)}, f32[2048,4]{0,1:T(4,128)S(1)}, /*index=5*/s32[]{:T(128)}, s32[]{:T(128)}) while((s32[]{:T(128)}, f32[8,512,4]{1,0,2:T(8,128)S(1)}, s32[8]{0:T(128)S(1)}, s32[2048]{0:T(1024)S(1)}, f32[2048,4]{0,1:T(4,128)S(1)}, ...), condition=%wide.region_12.13_spmd, body=%wide.region_11.12_spmd.sunk | while | flops 51380736 | bytes 86113 | solution.py:53
  240.0 1.9 fusion.90
  243.2 1.9 fusion.90
  246.5 1.9 fusion.90
  249.7 1.9 fusion.90
  253.0 1.9 fusion.90
  256.2 1.9 fusion.90
  259.5 1.9 fusion.90
  262.7 1.9 fusion.90
  266.0 1.2 reshape.151
  267.1 20.3 %all_to_all.13 = f32[128,1,128]{2,1,0:T(1,128)S(1)} all-to-all(f32[128,1,128]{2,1,0:T(1,128)S(1)} %reshape.151), channel_id=1, replica_groups=mesh['grp'=4,'cell'=128] {'cell'}, dimensions={0} | all-to-all | bytes 131072 | tf_op jit(solution)/shard_map/all_to_all | solution.py:142
  288.2 1.3 reshape.152
  290.4 5.6 %convert_reduce_fusion = (f32[4,256]{1,0:T(4,128)S(1)}, bf16[4,1024,256]{2,1,0:T(8,128)(2,1)S(1)}) fusion(f32[4,1024,256]{2,1,0:T(8,128)} %get-tuple-element.265, f32[4,256]{1,0:T(4,128)S(1)} %copy-done.13, f32[4,1024,4]{1,2,0:T(4,128)S(1)} %reshape.99, bf16[4,4,256]{2,1,0:T(4,128)(2,1)S(1)} %copy-done.8), kind=kOutput, calls=%fused_computation.30 | convolution fusion | flops 62913536 | bytes 6373376 | tf_op jit(solution)/shard_map/bnc,bch->bnh/dot_general | solution.py:151
  296.0 1.9 fusion.58
  298.5 1.9 convert_reduce_fusion.1
  300.4 1.3 fusion.28
  302.1 2.5 fusion.59
  304.6 15.7 %all-reduce.2 = (f32[4,256]{1,0:T(4,128)}, f32[4,256]{1,0:T(4,128)}, f32[4,4,256]{2,1,0:T(4,128)}, f32[4,4]{0,1:T(4,128)S(1)}) all-reduce(f32[4,256]{1,0:T(4,128)S(1)} %get-tuple-element.266, f32[4,256]{1,0:T(4,128)S(1)} %get-tuple-element.268, f32[4,4,256]{2,1,0:T(4,128)S(1)} %fusion.59, ...), channel_id=1, replica_groups=mesh['grp'=4,'cell'=128] {'grp'}, use_global_device_ids=true, to_apply=%region_15.16 | all-reduce | flops 6160 | bytes 49280 | tf_op jit(solution)/shard_map/psum | solution.py:171
  321.0 35.7 %all-reduce.6.cloned.1.call-done = (f32[4,96,256]{2,1,0:T(8,128)}, f32[4,256,256]{2,1,0:T(8,128)}) async-done(((f32[4,96,256]{2,1,0:T(8,128)}, f32[4,256,256]{2,1,0:T(8,128)}), (f32[4,96,256]{2,1,0:T(8,128)}, f32[4,256,256]{2,1,0:T(8,128)})) %all-reduce.6.cloned.1.call-update) | async-done | bytes 1441808 | tf_op jit(solution)/shard_map/psum | solution.py:171
  356.7 1.8 copy.121
  358.5 2.3 copy.122
  (196 shorter events, 31.4 us)
Async XLA Ops:
  7.2 175.2 %copy-start = (bf16[4,256,256]{2,1,0:T(8,128)(2,1)S(1)}, bf16[4,256,256]{2,1,0:T(8,128)(2,1)}, u32[]{:S(2)}) copy-start(bf16[4,256,256]{2,1,0:T(8,128)(2,1)} %param.26) | copy-start | bytes 1572868
  65.0 13.2 %copy-start.7 = (f32[3,32,64]{2,1,0:T(8,128)S(1)}, f32[3,32,64]{2,1,0:T(8,128)}, u32[]{:S(2)}) copy-start(f32[3,32,64]{2,1,0:T(8,128)} %param.20) | copy-start | bytes 73732
  106.3 72.9 %copy-start.12 = (bf16[4,96,256]{2,1,0:T(8,128)(2,1)S(1)}, bf16[4,96,256]{2,1,0:T(8,128)(2,1)}, u32[]{:S(2)}) copy-start(bf16[4,96,256]{2,1,0:T(8,128)(2,1)} %param.24) | copy-start | bytes 589828
  106.3 72.9 %copy-start.14 = (f32[4,256]{1,0:T(4,128)S(1)}, f32[4,256]{1,0:T(4,128)}, u32[]{:S(2)}) copy-start(f32[4,256]{1,0:T(4,128)} %param.25) | copy-start | bytes 12292
  179.3 3.1 copy-start.2
  179.3 3.1 copy-start.13
  182.4 3.2 copy-start.4
  182.4 4.6 %copy-start.8 = (bf16[4,4,256]{2,1,0:T(4,128)(2,1)S(1)}, bf16[4,4,256]{2,1,0:T(4,128)(2,1)}, u32[]{:S(2)}) copy-start(bf16[4,4,256]{2,1,0:T(4,128)(2,1)} %param.28) | copy-start | bytes 24580
  182.4 4.6 %copy-start.9 = (f32[4,4]{1,0:T(4,128)S(1)}, f32[4,4]{1,0:T(4,128)}, u32[]{:S(2)}) copy-start(f32[4,4]{1,0:T(4,128)} %param.29) | copy-start | bytes 196
  185.6 1.4 copy-start.1
  191.7 25.0 %all-to-all-start.1 = ((f32[128,1,128]{2,1,0:T(1,128)}), f32[128,1,128]{2,1,0:T(1,128)S(1)}, u32[]{:S(2)}, u32[]{:S(2)}) async-start(f32[128,1,128]{2,1,0:T(1,128)} %reshape.149), calls=%async_computation.1 | async-start | bytes 131072 | tf_op jit(solution)/shard_map/all_to_all | solution.py:129
  201.9 154.8 %all-reduce.6.cloned.1.call-start = ((), (), s32[]{:S(2)}) async-start(), calls=%async_computation.3 | async-start | bytes 2883584 | tf_op jit(solution)/shard_map/psum | solution.py:171
  221.6 16.1 %copy-start.6 = (f32[32,64]{1,0:T(8,128)S(1)}, f32[32,64]{1,0:T(8,128)}, u32[]{:S(2)}) copy-start(f32[32,64]{1,0:T(8,128)} %param.21) | copy-start | bytes 24580
  221.6 16.1 %copy-start.11 = (s32[32]{0:T(128)S(1)}, s32[32]{0:T(128)}, u32[]{:S(2)}) copy-start(s32[32]{0:T(128)} %param.22) | copy-start | bytes 388
  221.6 16.4 %copy-start.10 = (f32[3,32]{1,0:T(4,128)S(1)}, f32[3,32]{1,0:T(4,128)}, u32[]{:S(2)}) copy-start(f32[3,32]{1,0:T(4,128)} %param.23) | copy-start | bytes 1156
  290.4 5.6 %copy-start.5 = (bf16[4,1024,256]{2,1,0:T(8,128)(2,1)S(1)}, bf16[4,1024,256]{2,1,0:T(8,128)(2,1)}, u32[]{:S(2)}) copy-start(bf16[4,1024,256]{2,1,0:T(8,128)(2,1)} %copy-done.4) | copy-start | bytes 6291460
  296.0 2.6 copy-start.15
  298.5 1.9 copy-start.3
Sparse Core Ops, SparseCore 0:
  301.9 54.7 all-reduce.5
where the time goes:
time: 368 us
  blocking collectives  108 us (29%)
  local copies, waits for them, and re-layouts  103 us (28%)
  matrix products  58.2 us (16%)
  waiting for transfers between devices  50.3 us (14%)
  other arithmetic  21.8 us (6%)
  between operations  14.5 us (4%)
  starting transfers between devices  10.5 us (3%)
    all_to_all x1, blocking collectives, local(): lax.all_to_all(send_buf.reshape(local_blocks, cells, capacity, width), 'c...  72 us
    gather x12, local copies, waits for them, and re-layouts, local(): jnp.searchsorted(sorted_ids, jnp.arange(block_count, dtype=jnp.int32), si...  37.7 us
    psum x1, waiting for transfers between devices, local(): lax.psum((grad_first_weight, grad_first_bias, grad_second_weight, grad_se...  35.7 us
    dot_general x12, matrix products, table_product(): jnp.dot(onehot.astype(jnp.float32), values, precision=lax.Precision.HIGHE...  30.4 us
    all_to_all x1, blocking collectives, local(): lax.all_to_all(grad_buf.reshape(local_blocks, cells, capacity, channels),...  20.3 us
    psum x1, blocking collectives, local(): lax.psum((grad_first_weight, grad_first_bias, grad_second_weight, grad_se...  15.7 us
    unnamed x40, local copies, waits for them, and re-layouts  15.6 us
    all_to_all x1, waiting for transfers between devices, local(): lax.all_to_all(field_out.reshape(local_blocks, 1, cells * capacity, chann...  14.5 us
  transfers between devices with their start and end apart: 2, of which 2 were waited for; matrix products, arithmetic and copies ran while one was open for 1% of the time, Pallas kernels for 0%

commit v1 on v0

v1 whole, which is shorter than its diff:
```python
import functools
import math

import jax
import jax.numpy as jnp
from jax import lax
from jax.experimental import pallas as pl
from jax.experimental.pallas import tpu as pltpu
from jax.sharding import PartitionSpec as P

MESH = pl.DeviceIdType.MESH
F32 = jnp.float32
BF16 = jnp.bfloat16

CHANNELS = 4
RANKS = 8
LEVELS = 16
SINE = (6.283164044295505, -41.33714237020527, 81.34076885897593, -70.99343300945087)

NN = (((1,), (0,)), ((), ()))
NT = (((1,), (1,)), ((), ()))


def matmul(a, b, dims=NN):
    return lax.dot_general(a, b, dims, preferred_element_type=F32)


def turns_cosine(turns):
    rest = turns - jnp.round(turns)
    w = 0.25 - jnp.abs(rest)
    square = w * w
    poly = SINE[3]
    for coefficient in SINE[2::-1]:
        poly = poly * square + coefficient
    return w * poly


def split(values, parts):
    pieces = []
    for _ in range(parts - 1):
        piece = values.astype(BF16).astype(F32)
        pieces.append(piece)
        values = values - piece
    pieces.append(values)
    return pieces


def column(row):
    n = row.shape[1]
    diagonal = lax.broadcasted_iota(jnp.int32, (n, n), 0) == lax.broadcasted_iota(
        jnp.int32, (n, n), 1
    )
    return jnp.sum(jnp.where(diagonal, jnp.broadcast_to(row, (n, n)), 0.0), axis=1, keepdims=True)


def kernel(
    sizes,
    ids_ref,
    positions_ref,
    spacing_ref,
    lengths_ref,
    color_grad_ref,
    w1_ref,
    b1_ref,
    w2_ref,
    b2_ref,
    w3_ref,
    b3_ref,
    g1_out,
    g2_out,
    gs_out,
    v8,
    av,
    bt2,
    packed,
    bsend1,
    brecv1,
    asend1,
    arecv1,
    asend2,
    arecv2,
    bsend2,
    brecv2,
    bsend3,
    brecv3,
    asend3,
    arecv3,
    feat,
    act1,
    act2,
    slope1,
    slope2,
    delta1,
    delta2,
    og16,
    w1_own,
    w2_own,
    w1t,
    w2t,
    w3t,
    b2_wide,
    g1_own,
    g2_own,
    gs_own,
    load_sem,
    send_sem,
    recv_sem,
    own_sem,
):
    copies, group, levels_z, rays, samples = sizes
    inner = group // copies
    lanes = 2 * samples
    rows = rays // 2
    total = rays * samples
    width = levels_z * RANKS
    height = group * CHANNELS
    slots = group * width
    hidden = w2_own.shape[0]
    enc = w1_own.shape[0]

    y = lax.axis_index("grp")
    cell = lax.axis_index("cell")
    z = cell // inner
    inside = cell % inner
    me = y * inner + inside

    def device_a(peer):
        return {"grp": peer // inner, "cell": z * inner + peer % inner}

    def device_b(peer):
        return {"grp": y, "cell": peer * inner + inside}

    load1 = pltpu.make_async_copy(w1_ref.at[y], w1_own, load_sem.at[0])
    load2 = pltpu.make_async_copy(w2_ref.at[y], w2_own, load_sem.at[1])
    load1.start()
    load2.start()

    barrier = pltpu.get_barrier_semaphore()

    def greet_a(k, carry):
        pl.semaphore_signal(
            barrier, inc=1, device_id=device_a((me + k) % group), device_id_type=MESH
        )
        return carry

    def greet_b(k, carry):
        pl.semaphore_signal(
            barrier, inc=1, device_id=device_b((z + k) % levels_z), device_id_type=MESH
        )
        return carry

    lax.fori_loop(1, group, greet_a, 0)
    lax.fori_loop(1, levels_z, greet_b, 0)

    def exchange(source, target, index, own, count, device):
        target[own] = source[own]

        def send(k, carry):
            peer = (own + k) % count
            pltpu.make_async_remote_copy(
                src_ref=source.at[peer],
                dst_ref=target.at[own],
                send_sem=send_sem.at[index],
                recv_sem=recv_sem.at[index],
                device_id=device(peer),
                device_id_type=MESH,
            ).start()
            return carry

        lax.fori_loop(1, count, send, 0)
        others = target.at[pl.ds(0, count - 1)]
        pltpu.make_async_copy(others, others, recv_sem.at[index]).wait()

    def sent(source, index, count):
        others = source.at[pl.ds(0, count - 1)]
        pltpu.make_async_copy(others, others, send_sem.at[index]).wait()

    def exchange_a(source, target, index):
        exchange(source, target, index, me, group, device_a)

    def exchange_b(source, target, index):
        exchange(source, target, index, z, levels_z, device_b)

    def pair(values):
        return jnp.concatenate([values[:rows], values[rows:]], axis=1)

    ids = pair(ids_ref[...])
    ids_f = ids.astype(F32)
    square = ids_f
    if rows < lanes:
        square = jnp.concatenate([ids_f, jnp.full((lanes - rows, lanes), -1.0, F32)], axis=0)
    columns = square.T
    earlier = lax.broadcasted_iota(jnp.int32, (lanes, lanes), 0) < lax.broadcasted_iota(
        jnp.int32, (lanes, lanes), 1
    )
    id_rows = [ids_f[g : g + 1] for g in range(rows)]
    counts = [jnp.zeros((8, lanes), F32) for _ in range(rows)]
    for first in range(rows):
        wide = jnp.broadcast_to(columns[:, first : first + 1], (lanes, lanes))
        for g in range(first, rows):
            same = wide == id_rows[g]
            if g == first:
                same = same & earlier
            hits = jnp.where(same, 1.0, 0.0)
            counts[g] = counts[g] + jnp.sum(hits.reshape(lanes // 8, 8, lanes), axis=0)
    owner = ids // copies
    key_a = (ids % copies) * inner + owner % inner
    key_b = (owner // inner) * RANKS
    keys_a = [key_a[g : g + 1] for g in range(rows)]
    slot_row = lax.broadcasted_iota(jnp.int32, (width, lanes), 0)
    owner_row = lax.broadcasted_iota(jnp.int32, (height, lanes), 0) // CHANNELS
    for g in range(rows):
        rank = jnp.sum(counts[g], axis=0, keepdims=True).astype(jnp.int32)
        hit = jnp.where(slot_row == key_b[g : g + 1] + rank, 1.0, 0.0).astype(BF16)
        bt2[0:width, g * lanes : (g + 1) * lanes] = hit
        bt2[width : 2 * width, g * lanes : (g + 1) * lanes] = hit

    def spread(channels, parts):
        for c in range(CHANNELS):
            values = channels[c]
            v8[:, c, :] = values
            v8[:, c + CHANNELS, :] = values
        for g in range(rows):
            mine = owner_row == keys_a[g]
            for p, piece in enumerate(split(v8[g], parts)):
                tall = jnp.concatenate([piece] * (height // 8), axis=0)
                av[p * height : (p + 1) * height, g * lanes : (g + 1) * lanes] = jnp.where(
                    mine, tall, 0.0
                ).astype(BF16)
        wide = matmul(bt2[0:width], av[0 : parts * height], NT)
        result = wide[:, 0:height]
        for p in range(1, parts):
            result = result + wide[:, p * height : (p + 1) * height]
        return result

    def put_b(target, values):
        target[...] = values.reshape(levels_z, RANKS, height)

    def put_a(target, values):
        for j in range(group):
            target[j] = values[j * CHANNELS : (j + 1) * CHANNELS]

    def get_a(source):
        return jnp.concatenate([source[j] for j in range(group)], axis=0)

    positions = [pair(positions_ref[k]) for k in range(3)]
    put_b(bsend1, spread(positions + [jnp.zeros((rows, lanes), F32)], 3))

    pl.semaphore_wait(barrier, group - 1 + levels_z - 1)

    exchange_b(bsend1, brecv1, 0)
    put_a(asend1, brecv1[...].reshape(width, height).T)

    load1.wait()
    load2.wait()
    tall = feat.shape[0]
    b1 = b1_ref[pl.ds(y, 1), :]
    bias_rows = [piece for piece in split(b1, 3)]
    w1_all = jnp.concatenate(
        [w1_own[...].astype(F32)] + bias_rows + [jnp.zeros((tall - enc - 3, hidden), F32)], axis=0
    )
    w1t[...] = (w1_all * 0.5).T.astype(BF16)
    w2t[...] = (w2_own[...].astype(F32) * 0.5).T.astype(BF16)
    w3 = w3_ref[y].astype(F32)
    w3_tall = jnp.concatenate([w3, w3, jnp.zeros((lanes - 2 * CHANNELS, hidden), F32)], axis=0)
    w3t[...] = w3_tall.T[:, 0 : 4 * CHANNELS].astype(BF16)
    w3_rows = jnp.concatenate([w3, jnp.zeros((3 * CHANNELS, hidden), F32)], axis=0).astype(BF16)
    b2_wide[...] = jnp.broadcast_to(b2_ref[pl.ds(y, 1), :] * 0.5, (lanes, hidden)).T
    b3 = column(b3_ref[pl.ds(y, 1), :])
    one_row = lax.broadcasted_iota(jnp.int32, (tall - enc, slots), 0) < 3
    feat[enc:tall, :] = jnp.where(one_row, 1.0, 0.0).astype(BF16)
    act1[hidden:, :] = jnp.ones((act1.shape[0] - hidden, slots), BF16)

    exchange_a(asend1, arecv1, 1)

    level = lax.broadcasted_iota(jnp.int32, (3 * LEVELS, width), 0) % LEVELS
    half_turns = jnp.left_shift(1, level // 2).astype(F32) * jnp.where(
        level % 2 == 1, 0.5 * math.sqrt(2.0), 0.5
    )
    per_step = 4
    step_lanes = per_step * width

    def encode_step(j, carry):
        at = pl.ds(pl.multiple_of(j * width, width), width)
        point = arecv1[j]
        tall_point = jnp.concatenate(
            [jnp.broadcast_to(point[k : k + 1], (LEVELS, width)) for k in range(3)], axis=0
        )
        turns = tall_point * half_turns
        feat[0 : 3 * LEVELS, at] = turns_cosine(turns - 0.25).astype(BF16)
        feat[3 * LEVELS : 6 * LEVELS, at] = turns_cosine(turns).astype(BF16)
        return carry

    def activate(half, act, slope, at):
        bent = jnp.tanh(half)
        product = half * bent
        active = (half + product).astype(BF16)
        act[0:hidden, at] = active
        slope[:, at] = ((half + 1.0) - product) * (0.5 * bent + 0.5)
        return active

    def forward_step(i, carry):
        at = pl.ds(pl.multiple_of(i * step_lanes, step_lanes), step_lanes)
        first = activate(matmul(w1t[...], feat[:, at]), act1, slope1, at)
        bias = jnp.concatenate([b2_wide[...]] * (step_lanes // lanes), axis=1)
        second = activate(matmul(w2t[...], first) + bias, act2, slope2, at)
        out = matmul(w3_rows, second)[0:CHANNELS] + b3
        for k in range(per_step):
            asend2[i * per_step + k] = out[:, k * width : (k + 1) * width]
        return carry

    lax.fori_loop(0, group, encode_step, 0)
    lax.fori_loop(0, group // per_step, forward_step, 0)

    exchange_a(asend2, arecv2, 2)
    put_b(bsend2, get_a(arecv2).T)
    exchange_b(bsend2, brecv2, 3)
    returned = jnp.concatenate(split(brecv2[...].reshape(width, height).T, 2), axis=1).astype(BF16)
    for g in range(rows):
        at = slice(g * lanes, (g + 1) * lanes)
        found = matmul(returned, bt2[:, at])
        kept = jnp.where(owner_row == keys_a[g], found, 0.0)
        both = jnp.sum(kept.reshape(height // 8, 8, lanes), axis=0)
        v8[g] = both
    field = [v8[:, c, :] + v8[:, c + CHANNELS, :] for c in range(CHANNELS)]

    lane = lax.broadcasted_iota(jnp.int32, (rows, lanes), 1)
    left = lane < samples

    def per_ray(row):
        tall_row = column(row)
        return jnp.where(left, tall_row[:rows], tall_row[rows:])

    lengths = per_ray(lengths_ref[...].astype(F32))
    tint = [per_ray(color_grad_ref[c : c + 1, :]) for c in range(3)]
    spacing = pair(spacing_ref[...])
    before = lax.broadcasted_iota(jnp.int32, (lanes, lanes), 0)
    after = lax.broadcasted_iota(jnp.int32, (lanes, lanes), 1)
    same_ray = (before // samples) == (after // samples)

    def scan(values, mask):
        ones = jnp.where(mask & same_ray, 1.0, 0.0).astype(BF16)
        pieces = jnp.concatenate(split(values, 3), axis=0).astype(BF16)
        sums = matmul(pieces, ones)
        return sums[0:rows] + sums[rows : 2 * rows] + sums[2 * rows : 3 * rows]

    live = (lane % samples).astype(F32) < lengths
    density = jnp.maximum(field[0], 0.0) + jnp.log1p(jnp.exp(-jnp.abs(field[0])))
    step = jnp.where(live, density * spacing, 0.0)
    left_over = jnp.exp(-step)
    series = step * (
        1.0 - step * (1 / 2) * (1.0 - step * (1 / 3) * (1.0 - step * (1 / 4) * (1.0 - step * (1 / 5))))
    )
    absorbed = jnp.where(step < 0.05, series, 1.0 - left_over)
    trans = jnp.exp(-scan(step, before < after))
    weight = trans * absorbed
    shade = [0.5 + 0.5 * jnp.tanh(0.5 * field[c]) for c in range(1, CHANNELS)]
    seen = tint[0] * shade[0] + tint[1] * shade[1] + tint[2] * shade[2]
    behind = scan(weight * seen, before > after)
    step_grad = trans * left_over * seen - behind
    density_slope = 0.5 + 0.5 * jnp.tanh(0.5 * field[0])
    out_grad = [jnp.where(live, step_grad * spacing * density_slope, 0.0)]
    for c in range(3):
        out_grad.append(weight * tint[c] * shade[c] * (1.0 - shade[c]))

    put_b(bsend3, spread(out_grad, 2))
    exchange_b(bsend3, brecv3, 4)
    put_a(asend3, brecv3[...].reshape(width, height).T)
    exchange_a(asend3, arecv3, 5)

    def gather_step(j, carry):
        at = pl.ds(pl.multiple_of(j * width, width), width)
        grad = arecv3[j]
        packed[:, at] = grad
        og16[:, at] = jnp.concatenate(
            split(grad, 2) + [jnp.zeros((2 * CHANNELS, width), F32)], axis=0
        ).astype(BF16)
        return carry

    lax.fori_loop(0, group, gather_step, 0)

    def backward_second(i, carry):
        at = pl.ds(pl.multiple_of(i * step_lanes, step_lanes), step_lanes)
        delta2[:, at] = (matmul(w3t[...], og16[:, at]) * slope2[:, at]).astype(BF16)
        return carry

    lax.fori_loop(0, group // per_step, backward_second, 0)
    second = matmul(act1[...], delta2[...], NT)
    g2_own[...] = second[0:hidden].astype(BF16)

    def share(own, out, index):
        pltpu.make_async_copy(own, out.at[y], own_sem.at[index]).start()

        def send(k, carry):
            pltpu.make_async_remote_copy(
                src_ref=own,
                dst_ref=out.at[y],
                send_sem=send_sem.at[6 + index],
                recv_sem=recv_sem.at[6 + index],
                device_id={"grp": (y + k) % copies, "cell": cell},
                device_id_type=MESH,
            ).start()
            return carry

        lax.fori_loop(1, copies, send, 0)

    share(g2_own, g2_out, 0)

    def backward_first(i, carry):
        at = pl.ds(pl.multiple_of(i * step_lanes, step_lanes), step_lanes)
        delta1[:, at] = (matmul(w2_own[...], delta2[:, at]) * slope1[:, at]).astype(BF16)
        return carry

    lax.fori_loop(0, group // per_step, backward_first, 0)
    first = matmul(feat[...], delta1[...], NT)
    g1_own[...] = first[0:enc].astype(BF16)
    share(g1_own, g1_out, 1)
    third = matmul(og16[...], act2[...], NT)
    third_bias = jnp.sum(packed[...], axis=1, keepdims=True)
    gs_own[...] = jnp.concatenate(
        [
            first[enc : enc + 1],
            second[hidden : hidden + 1],
            jnp.zeros((2, hidden), F32),
            third[0:CHANNELS] + third[CHANNELS : 2 * CHANNELS],
            jnp.broadcast_to(third_bias, (CHANNELS, hidden)),
            jnp.zeros((4, hidden), F32),
        ],
        axis=0,
    )
    share(gs_own, gs_out, 2)

    for own, out, index in ((g2_own, g2_out, 0), (g1_own, g1_out, 1), (gs_own, gs_out, 2)):
        pltpu.make_async_copy(own, out.at[y], own_sem.at[index]).wait()
        others = out.at[pl.ds(0, copies - 1)]
        pltpu.make_async_copy(others, others, recv_sem.at[6 + index]).wait()
        pltpu.make_async_copy(others, others, send_sem.at[6 + index]).wait()
    sent(bsend1, 0, levels_z)
    sent(asend1, 1, group)
    sent(asend2, 2, group)
    sent(bsend2, 3, levels_z)
    sent(bsend3, 4, levels_z)
    sent(asend3, 5, group)


def local(levels_z, copies, *args):
    (ids, positions, spacing, lengths, color_grad, w1, b1, w2, b2, w3, b3) = args
    rays, samples = spacing.shape
    inner = lax.axis_size("cell") // levels_z
    group = copies * inner
    width = levels_z * RANKS
    height = group * CHANNELS
    slots = group * width
    blocks, enc, hidden = w1.shape
    total = rays * samples
    lanes = 2 * samples
    rows = rays // 2
    tall = enc + 16
    vmem = pl.BlockSpec(memory_space=pltpu.VMEM)
    hbm = pl.BlockSpec(memory_space=pl.ANY)
    part_a = pltpu.VMEM((group, CHANNELS, width), F32)
    part_b = pltpu.VMEM((levels_z, RANKS, height), F32)
    flops = 2 * slots * (3 * hidden * hidden + 3 * enc * hidden)
    g1, g2, gs = pl.pallas_call(
        functools.partial(kernel, (copies, group, levels_z, rays, samples)),
        out_shape=[
            jax.ShapeDtypeStruct((blocks, enc, hidden), BF16),
            jax.ShapeDtypeStruct((blocks, hidden, hidden), BF16),
            jax.ShapeDtypeStruct((blocks, 16, hidden), F32),
        ],
        in_specs=[vmem, vmem, vmem, vmem, vmem, hbm, vmem, hbm, vmem, vmem, vmem],
        out_specs=[hbm, hbm, hbm],
        scratch_shapes=[
            pltpu.VMEM((rows, 8, lanes), F32),
            pltpu.VMEM((3 * height, total), BF16),
            pltpu.VMEM((2 * width, total), BF16),
            pltpu.VMEM((CHANNELS, slots), F32),
            part_b,
            part_b,
            part_a,
            part_a,
            part_a,
            part_a,
            part_b,
            part_b,
            part_b,
            part_b,
            part_a,
            part_a,
            pltpu.VMEM((tall, slots), BF16),
            pltpu.VMEM((hidden + 16, slots), BF16),
            pltpu.VMEM((hidden, slots), BF16),
            pltpu.VMEM((hidden, slots), F32),
            pltpu.VMEM((hidden, slots), F32),
            pltpu.VMEM((hidden, slots), BF16),
            pltpu.VMEM((hidden, slots), BF16),
            pltpu.VMEM((4 * CHANNELS, slots), BF16),
            pltpu.VMEM((enc, hidden), BF16),
            pltpu.VMEM((hidden, hidden), BF16),
            pltpu.VMEM((hidden, tall), BF16),
            pltpu.VMEM((hidden, hidden), BF16),
            pltpu.VMEM((hidden, 4 * CHANNELS), BF16),
            pltpu.VMEM((hidden, lanes), F32),
            pltpu.VMEM((enc, hidden), BF16),
            pltpu.VMEM((hidden, hidden), BF16),
            pltpu.VMEM((16, hidden), F32),
            pltpu.SemaphoreType.DMA((2,)),
            pltpu.SemaphoreType.DMA((9,)),
            pltpu.SemaphoreType.DMA((9,)),
            pltpu.SemaphoreType.DMA((3,)),
        ],
        compiler_params=pltpu.CompilerParams(
            collective_id=0, has_side_effects=True, vmem_limit_bytes=48 * 1024 * 1024
        ),
        cost_estimate=pl.CostEstimate(flops=flops, bytes_accessed=1 << 21, transcendentals=slots * hidden * 2),
    )(
        ids.reshape(rays, samples),
        positions,
        spacing,
        lengths.reshape(1, rays),
        color_grad,
        w1,
        b1,
        w2,
        b2,
        w3,
        b3,
    )
    return (
        g1.astype(F32),
        gs[:, 0, :],
        g2.astype(F32),
        gs[:, 1, :],
        gs[:, 4:8, :],
        gs[:, 8:12, 0],
    )


def solution(mesh):
    copies, cells = mesh.shape["grp"], mesh.shape["cell"]
    levels_z = 16 if cells % 16 == 0 and cells >= 128 else 2
    in_specs = (
        P(("grp", "cell"), None, None),
        P(None, ("grp", "cell"), None),
        P(("grp", "cell"), None),
        P(("grp", "cell")),
        P(None, ("grp", "cell")),
        P("cell", None, None),
        P("cell", None),
        P("cell", None, None),
        P("cell", None),
        P("cell", None, None),
        P("cell", None),
    )
    out_specs = (
        P("cell", None, None),
        P("cell", None),
        P("cell", None, None),
        P("cell", None),
        P("cell", None, None),
        P("cell", None),
    )
    return jax.shard_map(
        functools.partial(local, levels_z, copies),
        mesh=mesh,
        in_specs=in_specs,
        out_specs=out_specs,
        check_vma=False,
    )
```

time: 368 us -> 90.2 us (0.25)
  blocking collectives: 108 us -> 0 us
  local copies, waits for them, and re-layouts: 103 us -> 9.5 us
  Pallas kernels: 0 us -> 77.7 us
  matrix products: 58.2 us -> 0 us
  waiting for transfers between devices: 50.3 us -> 0 us
  other arithmetic: 21.8 us -> 1.83 us
  between operations: 14.5 us -> 0.68 us
  starting transfers between devices: 10.5 us -> 0 us
    all_to_all x2 -> x0, blocking collectives: 92.3 us -> none  [the longest x1 72 us: local(): lax.all_to_all(send_buf.reshape(local_blocks, cells, capacity, width), 'c...]
    pallas_call x0 -> x1, Pallas kernels: none -> 77.7 us  [local(): pl.pallas_call(functools.partial(kernel, (copies, group, levels_z, rays,...]
    gather x14 -> x0, local copies, waits for them, and re-layouts: 62.7 us -> none  [the longest x12 37.7 us: local(): jnp.searchsorted(sorted_ids, jnp.arange(block_count, dtype=jnp.int32), si...]
    dot_general x28 -> x0, matrix products: 58.2 us -> none  [the longest x12 30.4 us: table_product(): jnp.dot(onehot.astype(jnp.float32), values, precision=lax.Precision.HIGHE...]
    psum x1 -> x0, waiting for transfers between devices: 35.7 us -> none  [local(): lax.psum((grad_first_weight, grad_first_bias, grad_second_weight, grad_se...]
    psum x1 -> x0, blocking collectives: 15.7 us -> none  [local(): lax.psum((grad_first_weight, grad_first_bias, grad_second_weight, grad_se...]
    all_to_all x1 -> x0, waiting for transfers between devices: 14.5 us -> none  [local(): lax.all_to_all(field_out.reshape(local_blocks, 1, cells * capacity, chann...]
    add x29 -> x0, other arithmetic: 10.5 us -> none  [the longest x16 10.3 us: place_block(): targets = start + jnp.arange(step, dtype=jnp.int32)]
  transfers between devices with their start and end apart: 2 -> 0, of which waited for: 2 -> 0; matrix products, arithmetic and copies ran while one was open for 1% -> 0% of each run, Pallas kernels for 0% -> 0%
where the time goes in v1:
time: 90.2 us; the launch traced here: 89.7 us
  Pallas kernels  77.7 us (86%)
  local copies, waits for them, and re-layouts  9.5 us (11%)
  other arithmetic  1.83 us (2%)
    pallas_call x1, Pallas kernels, local(): pl.pallas_call(functools.partial(kernel, (copies, group, levels_z, rays,...  77.7 us
    unnamed x23, local copies, waits for them, and re-layouts  8.22 us

profile of v1, /device:TPU:1, one launch (start us, length us, event | category | flops | bytes accessed | tf_op | source)
XLA Modules:
  0.0 89.7 jit_solution(1147049320947442082)
XLA Ops:
  0.6 0.0 copy-start.8
  0.6 0.0 copy-start.10
  0.7 0.7 copy-done.8
  1.3 0.0 copy-done.10
  1.3 0.0 copy-start
  1.3 1.0 %copy-done = bf16[4,256,256]{2,1,0:T(8,128)(2,1)S(1)} copy-done((bf16[4,256,256]{2,1,0:T(8,128)(2,1)S(1)}, bf16[4,256,256]{2,1,0:T(8,128)(2,1)}, u32[]{:S(2)}) %copy-start) | copy-done | bytes 524312
  2.4 0.0 copy-start.1
  2.4 0.9 %copy-done.1 = bf16[4,96,256]{2,1,0:T(8,128)(2,1)S(1)} copy-done((bf16[4,96,256]{2,1,0:T(8,128)(2,1)S(1)}, bf16[4,96,256]{2,1,0:T(8,128)(2,1)}, u32[]{:S(2)}) %copy-start.1) | copy-done | bytes 196632
  3.3 0.0 copy-start.2
  3.3 0.8 copy-done.2
  4.1 0.0 copy-start.3
  4.1 0.7 copy-done.3
  4.8 0.0 copy-start.4
  4.8 0.7 copy-done.4
  5.5 0.0 copy-start.5
  5.5 0.7 copy-done.5
  6.2 0.0 copy-start.6
  6.2 0.7 copy-done.6
  6.9 0.0 copy-start.7
  6.9 0.7 copy-done.7
  7.6 0.0 copy-start.9
  7.6 0.7 copy-done.9
  8.3 77.7 %shard_map.154 = (bf16[4,96,256]{2,1,0:T(8,128)(2,1)S(1)}, bf16[4,256,256]{2,1,0:T(8,128)(2,1)S(1)}, f32[4,16,256]{2,1,0:T(8,128)S(1)}) custom-call(s32[32,64]{1,0:T(8,128)S(1)} %bitcast.6, f32[3,32,64]{2,1,0:T(8,128)S(1)} %copy-done.2, f32[32,64]{1,0:T(8,128)S(1)} %copy-done.4, s32[1,32]{1,0:T(1,128)S(1)} %bitcast.7, f32[3,32]{1,0:T(4,128)S(1)} %copy-done.8, ...), custom_call_target="tpu_custom_call" | custom-call | flops 2214592512 | bytes 2097152 | tf_op jit(solution)/shard_map/pallas_call | solution.py:464
  86.0 0.6 copy_bitcast_fusion
  86.6 0.6 slice.14
  87.2 0.7 slice_reduce_fusion
  87.8 1.1 %convert_element_type.7 = f32[4,256,256]{2,1,0:T(8,128)} convert(bf16[4,256,256]{2,1,0:T(8,128)(2,1)S(1)} %get-tuple-element.11) | non-fusion elementwise | flops 262144 | bytes 1572864 | tf_op jit(solution)/shard_map/convert_element_type | solution.py:532
  88.9 0.8 convert_element_type.6
  (1 shorter events, 0.0 us)
Async XLA Ops:
  0.6 0.7 copy-start.8
  0.6 0.7 copy-start.10
  1.3 1.0 %copy-start = (bf16[4,256,256]{2,1,0:T(8,128)(2,1)S(1)}, bf16[4,256,256]{2,1,0:T(8,128)(2,1)}, u32[]{:S(2)}) copy-start(bf16[4,256,256]{2,1,0:T(8,128)(2,1)} %w2_ref.1) | copy-start | bytes 1572868
  2.4 0.9 %copy-start.1 = (bf16[4,96,256]{2,1,0:T(8,128)(2,1)S(1)}, bf16[4,96,256]{2,1,0:T(8,128)(2,1)}, u32[]{:S(2)}) copy-start(bf16[4,96,256]{2,1,0:T(8,128)(2,1)} %w1_ref.1) | copy-start | bytes 589828
  3.3 0.8 copy-start.2
  4.1 0.7 copy-start.3
  4.8 0.7 copy-start.4
  5.5 0.7 copy-start.5
  6.2 0.7 copy-start.6
  6.9 0.7 copy-start.7
  7.6 0.7 copy-start.9

commit v2 on v1

--- a/solution.py
+++ b/solution.py
@@ -15,6 +15,7 @@
 CHANNELS = 4
 RANKS = 8
 LEVELS = 16
+VMEM_BYTES = 64 * 1024 * 1024 - 64 * 1024
 SINE = (6.283164044295505, -41.33714237020527, 81.34076885897593, -70.99343300945087)
 
 NN = (((1,), (0,)), ((), ()))
@@ -53,38 +54,61 @@
     return jnp.sum(jnp.where(diagonal, jnp.broadcast_to(row, (n, n)), 0.0), axis=1, keepdims=True)
 
 
+def swap(tiles):
+    lanes = tiles.shape[2]
+    part = lanes // 8
+    sub = lax.broadcasted_iota(jnp.int32, tiles.shape, 1)
+    lane = lax.broadcasted_iota(jnp.int32, tiles.shape, 2) // part
+    for bit in (1, 2, 4):
+        low = pltpu.roll(pltpu.roll(tiles, 8 - bit, 1), bit * part, 2)
+        high = pltpu.roll(pltpu.roll(tiles, bit, 1), lanes - bit * part, 2)
+        sub_set = (sub & bit) != 0
+        lane_set = (lane & bit) != 0
+        moved = jnp.where(lane_set, low, high)
+        tiles = jnp.where(sub_set == lane_set, tiles, moved)
+    return tiles
+
+
 def kernel(
     sizes,
+    ids_hbm,
+    positions_hbm,
+    spacing_hbm,
+    lengths_hbm,
+    color_grad_hbm,
+    w1_hbm,
+    b1_hbm,
+    w2_hbm,
+    b2_hbm,
+    w3_hbm,
+    b3_hbm,
+    g1_out,
+    g2_out,
+    gs_out,
     ids_ref,
     positions_ref,
     spacing_ref,
     lengths_ref,
     color_grad_ref,
-    w1_ref,
     b1_ref,
-    w2_ref,
     b2_ref,
     w3_ref,
     b3_ref,
-    g1_out,
-    g2_out,
-    gs_out,
     v8,
     av,
     bt2,
-    packed,
+    asend1,
+    arecv1,
     bsend1,
     brecv1,
-    asend1,
-    arecv1,
+    bsend2,
+    brecv2,
     asend2,
     arecv2,
-    bsend2,
-    brecv2,
+    asend3,
+    arecv3,
     bsend3,
     brecv3,
-    asend3,
-    arecv3,
     feat,
     act1,
     act2,
@@ -93,6 +117,8 @@
     delta1,
     delta2,
     og16,
+    og_sum,
+    second_sum,
     w1_own,
     w2_own,
     w1t,
@@ -105,6 +131,7 @@
     load_sem,
     send_sem,
     recv_sem,
+    near_sem,
     own_sem,
 ):
     copies, group, levels_z, rays, samples = sizes
@@ -130,11 +157,6 @@
     def device_b(peer):
         return {"grp": y, "cell": peer * inner + inside}
 
-    load1 = pltpu.make_async_copy(w1_ref.at[y], w1_own, load_sem.at[0])
-    load2 = pltpu.make_async_copy(w2_ref.at[y], w2_own, load_sem.at[1])
-    load1.start()
-    load2.start()
-
     barrier = pltpu.get_barrier_semaphore()
 
     def greet_a(k, carry):
@@ -143,43 +165,77 @@
         )
         return carry
 
+    def far_first(k):
+        left = levels_z - k
+        odd = left % 2
+        return (z + odd * ((left + 1) // 2) + (1 - odd) * (levels_z - left // 2)) % levels_z
+
     def greet_b(k, carry):
-        pl.semaphore_signal(
-            barrier, inc=1, device_id=device_b((z + k) % levels_z), device_id_type=MESH
+        pl.semaphore_signal(barrier, inc=1, device_id=device_b(far_first(k)), device_id_type=MESH)
+        return carry
+
+    lax.fori_loop(1, levels_z, greet_b, 0)
+    lax.fori_loop(1, group, greet_a, 0)
+
+    loads = [
+        pltpu.make_async_copy(source, target, load_sem.at[i])
+        for i, (source, target) in enumerate(
+            (
+                (ids_hbm, ids_ref),
+                (positions_hbm, positions_ref),
+                (w2_hbm.at[y], w2_own),
+                (w1_hbm.at[y], w1_own),
+                (b1_hbm, b1_ref),
+                (b2_hbm, b2_ref),
+                (w3_hbm, w3_ref),
+                (b3_hbm, b3_ref),
+                (spacing_hbm, spacing_ref),
+                (lengths_hbm, lengths_ref),
+                (color_grad_hbm, color_grad_ref),
+            )
         )
-        return carry
-
-    lax.fori_loop(1, group, greet_a, 0)
-    lax.fori_loop(1, levels_z, greet_b, 0)
-
-    def exchange(source, target, index, own, count, device):
-        target[own] = source[own]
-
-        def send(k, carry):
-            peer = (own + k) % count
-            pltpu.make_async_remote_copy(
-                src_ref=source.at[peer],
-                dst_ref=target.at[own],
-                send_sem=send_sem.at[index],
-                recv_sem=recv_sem.at[index],
-                device_id=device(peer),
-                device_id_type=MESH,
-            ).start()
+    ]
+    for load in loads:
+        load.start()
+    loads[0].wait()
+
+    def send(source, target, index, own, peer, device, arrived):
+        pltpu.make_async_remote_copy(
+            src_ref=source.at[peer],
+            dst_ref=target.at[own],
+            send_sem=send_sem.at[index],
+            recv_sem=arrived,
+            device_id=device,
+            device_id_type=MESH,
+        ).start()
+
+    def wait_all(buffer, count, sem):
+        others = buffer.at[pl.ds(0, count - 1)]
+        pltpu.make_async_copy(others, others, sem).wait()
+
+    def exchange_a(source, target, index):
+        target[me] = source[me]
+
+        def step(k, carry):
+            peer = (me + k) % group
+            send(source, target, index, me, peer, device_a(peer), recv_sem.at[index])
             return carry
 
-        lax.fori_loop(1, count, send, 0)
-        others = target.at[pl.ds(0, count - 1)]
-        pltpu.make_async_copy(others, others, recv_sem.at[index]).wait()
-
-    def sent(source, index, count):
-        others = source.at[pl.ds(0, count - 1)]
-        pltpu.make_async_copy(others, others, send_sem.at[index]).wait()
-
-    def exchange_a(source, target, index):
-        exchange(source, target, index, me, group, device_a)
-
-    def exchange_b(source, target, index):
-        exchange(source, target, index, z, levels_z, device_b)
+        lax.fori_loop(1, group, step, 0)
+        wait_all(target, group, recv_sem.at[index])
+
+    def send_b(source, target, index, row):
+        target[z] = source[z]
+
+        def step(k, carry):
+            peer = far_first(k)
+            send(source, target, index, z, peer, device_b(peer), near_sem.at[row, z])
+            return carry
+
+        lax.fori_loop(1, levels_z, step, 0)
+
+    def arrival(target, row, peer):
+        pltpu.make_async_copy(target.at[peer], target.at[peer], near_sem.at[row, peer]).wait()
 
     def pair(values):
         return jnp.concatenate([values[:rows], values[rows:]], axis=1)
@@ -227,14 +283,13 @@
                 av[p * height : (p + 1) * height, g * lanes : (g + 1) * lanes] = jnp.where(
                     mine, tall, 0.0
                 ).astype(BF16)
-        wide = matmul(bt2[0:width], av[0 : parts * height], NT)
-        result = wide[:, 0:height]
+        wide = matmul(av[0 : parts * height], bt2[0:width], NT)
+        result = wide[0:height]
         for p in range(1, parts):
-            result = result + wide[:, p * height : (p + 1) * height]
+            result = result + wide[p * height : (p + 1) * height]
         return result
 
-    def put_b(target, values):
-        target[...] = values.reshape(levels_z, RANKS, height)
+    half = group // 2
 
     def put_a(target, values):
         for j in range(group):
@@ -243,16 +298,30 @@
     def get_a(source):
         return jnp.concatenate([source[j] for j in range(group)], axis=0)
 
+    def a_to_b(arrived, target):
+        tall = jnp.concatenate(
+            [
+                arrived[h * half : (h + 1) * half, c, :]
+                for h in range(2)
+                for c in range(CHANNELS)
+            ],
+            axis=0,
+        )
+        target[...] = swap(tall.T.reshape(levels_z, RANKS, height))
+
+    def b_to_a(arrived, target):
+        tall = swap(arrived[...]).reshape(width, height).T
+        for h in range(2):
+            for c in range(CHANNELS):
+                at = (h * CHANNELS + c) * half
+                target[h * half : (h + 1) * half, c, :] = tall[at : at + half]
+
+    loads[1].wait()
     positions = [pair(positions_ref[k]) for k in range(3)]
-    put_b(bsend1, spread(positions + [jnp.zeros((rows, lanes), F32)], 3))
-
-    pl.semaphore_wait(barrier, group - 1 + levels_z - 1)
-
-    exchange_b(bsend1, brecv1, 0)
-    put_a(asend1, brecv1[...].reshape(width, height).T)
-
-    load1.wait()
-    load2.wait()
+    put_a(asend1, spread(positions + [jnp.zeros((rows, lanes), F32)], 3))
+
+    for load in loads[2:]:
+        load.wait()
     tall = feat.shape[0]
     b1 = b1_ref[pl.ds(y, 1), :]
     bias_rows = [piece for piece in split(b1, 3)]
@@ -271,25 +340,49 @@
     feat[enc:tall, :] = jnp.where(one_row, 1.0, 0.0).astype(BF16)
     act1[hidden:, :] = jnp.ones((act1.shape[0] - hidden, slots), BF16)
 
-    exchange_a(asend1, arecv1, 1)
-
-    level = lax.broadcasted_iota(jnp.int32, (3 * LEVELS, width), 0) % LEVELS
+    second_sum[...] = jnp.zeros(second_sum.shape, F32)
+    og_sum[...] = jnp.zeros(og_sum.shape, F32)
+
+    pl.semaphore_wait(barrier, group - 1 + levels_z - 1)
+    exchange_a(asend1, arecv1, 0)
+    a_to_b(arecv1, bsend1)
+    send_b(bsend1, brecv1, 1, 0)
+
+    lane_tile = height
+    level = lax.broadcasted_iota(jnp.int32, (3 * LEVELS, lane_tile), 0) % LEVELS
     half_turns = jnp.left_shift(1, level // 2).astype(F32) * jnp.where(
         level % 2 == 1, 0.5 * math.sqrt(2.0), 0.5
     )
-    per_step = 4
-    step_lanes = per_step * width
-
-    def encode_step(j, carry):
-        at = pl.ds(pl.multiple_of(j * width, width), width)
-        point = arecv1[j]
-        tall_point = jnp.concatenate(
-            [jnp.broadcast_to(point[k : k + 1], (LEVELS, width)) for k in range(3)], axis=0
-        )
-        turns = tall_point * half_turns
-        feat[0 : 3 * LEVELS, at] = turns_cosine(turns - 0.25).astype(BF16)
-        feat[3 * LEVELS : 6 * LEVELS, at] = turns_cosine(turns).astype(BF16)
-        return carry
+    step_lanes = 4 * lane_tile
+
+    def sources(i):
+        return (z + levels_z - i) % levels_z, (z + i + 1) % levels_z
+
+    def arrivals(target, row, i):
+        first, second = sources(i)
+
+        @pl.when(i > 0)
+        def _():
+            arrival(target, row, first)
+
+        arrival(target, row, second)
+        return first, second
+
+    def encode(point, start):
+        for h in range(2):
+            at = pl.ds(pl.multiple_of(start + h * lane_tile, lane_tile), lane_tile)
+            tall_point = jnp.concatenate(
+                [
+                    jnp.broadcast_to(
+                        point[h * CHANNELS + k : h * CHANNELS + k + 1], (LEVELS, lane_tile)
+                    )
+                    for k in range(3)
+                ],
+                axis=0,
+            )
+            turns = tall_point * half_turns
+            feat[0 : 3 * LEVELS, at] = turns_cosine(turns - 0.25).astype(BF16)
+            feat[3 * LEVELS : 6 * LEVELS, at] = turns_cosine(turns).astype(BF16)
 
     def activate(half, act, slope, at):
         bent = jnp.tanh(half)
@@ -300,22 +393,39 @@
         return active
 
     def forward_step(i, carry):
-        at = pl.ds(pl.multiple_of(i * step_lanes, step_lanes), step_lanes)
+        start = i * step_lanes
+        at = pl.ds(pl.multiple_of(start, step_lanes), step_lanes)
+        pair_of = arrivals(brecv1, 0, i)
+        for s, source in enumerate(pair_of):
+            encode(brecv1[source], start + 2 * s * lane_tile)
         first = activate(matmul(w1t[...], feat[:, at]), act1, slope1, at)
         bias = jnp.concatenate([b2_wide[...]] * (step_lanes // lanes), axis=1)
         second = activate(matmul(w2t[...], first) + bias, act2, slope2, at)
         out = matmul(w3_rows, second)[0:CHANNELS] + b3
-        for k in range(per_step):
-            asend2[i * per_step + k] = out[:, k * width : (k + 1) * width]
+        for s, source in enumerate(pair_of):
+            base = 2 * s * lane_tile
+            bsend2[source] = jnp.concatenate(
+                [
+                    out[:, base : base + lane_tile],
+                    out[:, base + lane_tile : base + 2 * lane_tile],
+                ],
+                axis=0,
+            )
+
+        @pl.when(i > 0)
+        def _():
+            send(bsend2, brecv2, 2, z, pair_of[0], device_b(pair_of[0]), recv_sem.at[2])
+
+        send(bsend2, brecv2, 2, z, pair_of[1], device_b(pair_of[1]), recv_sem.at[2])
         return carry
 
-    lax.fori_loop(0, group, encode_step, 0)
-    lax.fori_loop(0, group // per_step, forward_step, 0)
-
-    exchange_a(asend2, arecv2, 2)
-    put_b(bsend2, get_a(arecv2).T)
-    exchange_b(bsend2, brecv2, 3)
-    returned = jnp.concatenate(split(brecv2[...].reshape(width, height).T, 2), axis=1).astype(BF16)
+    lax.fori_loop(0, levels_z // 2, forward_step, 0)
+
+    brecv2[z] = bsend2[z]
+    wait_all(brecv2, levels_z, recv_sem.at[2])
+    b_to_a(brecv2, asend2)
+    exchange_a(asend2, arecv2, 3)
+    returned = jnp.concatenate(split(get_a(arecv2), 2), axis=1).astype(BF16)
     for g in range(rows):
         at = slice(g * lanes, (g + 1) * lanes)
         found = matmul(returned, bt2[:, at])
@@ -363,29 +473,31 @@
     for c in range(3):
         out_grad.append(weight * tint[c] * shade[c] * (1.0 - shade[c]))
 
-    put_b(bsend3, spread(out_grad, 2))
-    exchange_b(bsend3, brecv3, 4)
-    put_a(asend3, brecv3[...].reshape(width, height).T)
-    exchange_a(asend3, arecv3, 5)
-
-    def gather_step(j, carry):
-        at = pl.ds(pl.multiple_of(j * width, width), width)
-        grad = arecv3[j]
-        packed[:, at] = grad
-        og16[:, at] = jnp.concatenate(
-            split(grad, 2) + [jnp.zeros((2 * CHANNELS, width), F32)], axis=0
+    put_a(asend3, spread(out_grad, 2))
+    exchange_a(asend3, arecv3, 4)
+    a_to_b(arecv3, bsend3)
+    send_b(bsend3, brecv3, 5, 1)
+
+    def backward_second(i, carry):
+        start = i * step_lanes
+        at = pl.ds(pl.multiple_of(start, step_lanes), step_lanes)
+        pair_of = arrivals(brecv3, 1, i)
+        tiles = [brecv3[source] for source in pair_of]
+        og_sum[...] = og_sum[...] + (tiles[0] + tiles[1])
+        grad = jnp.concatenate(
+            [tile[h * CHANNELS : (h + 1) * CHANNELS] for tile in tiles for h in range(2)], axis=1
+        )
+        pieces = jnp.concatenate(
+            split(grad, 2) + [jnp.zeros((2 * CHANNELS, step_lanes), F32)], axis=0
         ).astype(BF16)
+        og16[:, at] = pieces
+        delta = (matmul(w3t[...], pieces) * slope2[:, at]).astype(BF16)
+        delta2[:, at] = delta
+        second_sum[...] = second_sum[...] + matmul(act1[:, at], delta, NT)
         return carry
 
-    lax.fori_loop(0, group, gather_step, 0)
-
-    def backward_second(i, carry):
-        at = pl.ds(pl.multiple_of(i * step_lanes, step_lanes), step_lanes)
-        delta2[:, at] = (matmul(w3t[...], og16[:, at]) * slope2[:, at]).astype(BF16)
-        return carry
-
-    lax.fori_loop(0, group // per_step, backward_second, 0)
-    second = matmul(act1[...], delta2[...], NT)
+    lax.fori_loop(0, levels_z // 2, backward_second, 0)
+    second = second_sum[...]
     g2_own[...] = second[0:hidden].astype(BF16)
 
     def share(own, out, index):
@@ -411,20 +523,29 @@
         delta1[:, at] = (matmul(w2_own[...], delta2[:, at]) * slope1[:, at]).astype(BF16)
         return carry
 
-    lax.fori_loop(0, group // per_step, backward_first, 0)
+    lax.fori_loop(0, levels_z // 2, backward_first, 0)
     first = matmul(feat[...], delta1[...], NT)
     g1_own[...] = first[0:enc].astype(BF16)
     share(g1_own, g1_out, 1)
     third = matmul(og16[...], act2[...], NT)
-    third_bias = jnp.sum(packed[...], axis=1, keepdims=True)
+    og_total = jnp.sum(og_sum[...], axis=1, keepdims=True)
+    og_total = og_total[0:CHANNELS] + og_total[CHANNELS : 2 * CHANNELS]
+    diagonal = lax.broadcasted_iota(jnp.int32, (CHANNELS, hidden), 0) == lax.broadcasted_iota(
+        jnp.int32, (CHANNELS, hidden), 1
+    )
+    third_bias = jnp.sum(
+        jnp.where(diagonal, jnp.broadcast_to(og_total, (CHANNELS, hidden)), 0.0),
+        axis=0,
+        keepdims=True,
+    )
     gs_own[...] = jnp.concatenate(
         [
             first[enc : enc + 1],
             second[hidden : hidden + 1],
             jnp.zeros((2, hidden), F32),
             third[0:CHANNELS] + third[CHANNELS : 2 * CHANNELS],
-            jnp.broadcast_to(third_bias, (CHANNELS, hidden)),
-            jnp.zeros((4, hidden), F32),
+            third_bias,
+            jnp.zeros((7, hidden), F32),
         ],
         axis=0,
     )
@@ -432,15 +553,53 @@
 
     for own, out, index in ((g2_own, g2_out, 0), (g1_own, g1_out, 1), (gs_own, gs_out, 2)):
         pltpu.make_async_copy(own, out.at[y], own_sem.at[index]).wait()
-        others = out.at[pl.ds(0, copies - 1)]
-        pltpu.make_async_copy(others, others, recv_sem.at[6 + index]).wait()
-        pltpu.make_async_copy(others, others, send_sem.at[6 + index]).wait()
-    sent(bsend1, 0, levels_z)
-    sent(asend1, 1, group)
-    sent(asend2, 2, group)
-    sent(bsend2, 3, levels_z)
-    sent(bsend3, 4, levels_z)
-    sent(asend3, 5, group)
+        wait_all(out, copies, recv_sem.at[6 + index])
+        wait_all(out, copies, send_sem.at[6 + index])
+    wait_all(asend1, group, send_sem.at[0])
+    wait_all(bsend1, levels_z, send_sem.at[1])
+    wait_all(bsend2, levels_z, send_sem.at[2])
+    wait_all(asend2, group, send_sem.at[3])
+    wait_all(asend3, group, send_sem.at[4])
+    wait_all(bsend3, levels_z, send_sem.at[5])
+
+
+def finish(
+    g1, g2, gs, g1_out, b1_out, g2_out, b2_out, g3_out, b3_out,
+    g1_b, g2_b, gs_b, g1_f, b1_f, g2_f, b2_f, g3_f, b3_f, load_sems, sems
+):
+    copies = []
+
+    def put(source, target):
+        copy = pltpu.make_async_copy(source, target, sems.at[len(copies)])
+        copy.start()
+        copies.append(copy)
+
+    blocks = g1.shape[0]
+    loads = [pltpu.make_async_copy(gs, gs_b, load_sems.at[2 * blocks])]
+    for b in range(blocks):
+        loads.append(pltpu.make_async_copy(g2.at[b], g2_b.at[b], load_sems.at[2 * b]))
+        loads.append(pltpu.make_async_copy(g1.at[b], g1_b.at[b], load_sems.at[2 * b + 1]))
+    for load in loads:
+        load.start()
+    loads[0].wait()
+    for b in range(blocks):
+        b1_f[b : b + 1, :] = gs_b[b, 0:1, :]
+        b2_f[b : b + 1, :] = gs_b[b, 1:2, :]
+        g3_f[b] = gs_b[b, 4:8, :]
+        b3_f[b : b + 1, :] = gs_b[b, 8:9, 0 : b3_f.shape[1]]
+    put(b1_f, b1_out)
+    put(b2_f, b2_out)
+    put(g3_f, g3_out)
+    put(b3_f, b3_out)
+    for b in range(blocks):
+        loads[1 + 2 * b].wait()
+        g2_f[b] = g2_b[b].astype(F32)
+        put(g2_f.at[b], g2_out.at[b])
+        loads[2 + 2 * b].wait()
+        g1_f[b] = g1_b[b].astype(F32)
+        put(g1_f.at[b], g1_out.at[b])
+    for copy in copies:
+        copy.wait()
 
 
 def local(levels_z, copies, *args):
@@ -456,8 +615,7 @@
     lanes = 2 * samples
     rows = rays // 2
     tall = enc + 16
-    vmem = pl.BlockSpec(memory_space=pltpu.VMEM)
-    hbm = pl.BlockSpec(memory_space=pl.ANY)
+    hbm = pl.BlockSpec(memory_space=pltpu.HBM)
     part_a = pltpu.VMEM((group, CHANNELS, width), F32)
     part_b = pltpu.VMEM((levels_z, RANKS, height), F32)
     flops = 2 * slots * (3 * hidden * hidden + 3 * enc * hidden)
@@ -468,13 +626,25 @@
             jax.ShapeDtypeStruct((blocks, hidden, hidden), BF16),
             jax.ShapeDtypeStruct((blocks, 16, hidden), F32),
         ],
-        in_specs=[vmem, vmem, vmem, vmem, vmem, hbm, vmem, hbm, vmem, vmem, vmem],
-        out_specs=[hbm, hbm, hbm],
+        in_specs=[hbm] * 11,
+        out_specs=[hbm] * 3,
         scratch_shapes=[
+            pltpu.VMEM((rays, samples), jnp.int32),
+            pltpu.VMEM((3, rays, samples), F32),
+            pltpu.VMEM((rays, samples), F32),
+            pltpu.VMEM((1, rays), jnp.int32),
+            pltpu.VMEM((3, rays), F32),
+            pltpu.VMEM(b1.shape, F32),
+            pltpu.VMEM(b2.shape, F32),
+            pltpu.VMEM(w3.shape, BF16),
+            pltpu.VMEM(b3.shape, F32),
             pltpu.VMEM((rows, 8, lanes), F32),
             pltpu.VMEM((3 * height, total), BF16),
             pltpu.VMEM((2 * width, total), BF16),
-            pltpu.VMEM((CHANNELS, slots), F32),
+            part_a,
+            part_a,
+            part_b,
+            part_b,
             part_b,
             part_b,
             part_a,
@@ -483,10 +653,6 @@
             part_a,
             part_b,
             part_b,
-            part_b,
-            part_b,
-            part_a,
-            part_a,
             pltpu.VMEM((tall, slots), BF16),
             pltpu.VMEM((hidden + 16, slots), BF16),
             pltpu.VMEM((hidden, slots), BF16),
@@ -495,6 +661,8 @@
             pltpu.VMEM((hidden, slots), BF16),
             pltpu.VMEM((hidden, slots), BF16),
             pltpu.VMEM((4 * CHANNELS, slots), BF16),
+            pltpu.VMEM((8, height), F32),
+            pltpu.VMEM((hidden + 16, hidden), F32),
             pltpu.VMEM((enc, hidden), BF16),
             pltpu.VMEM((hidden, hidden), BF16),
             pltpu.VMEM((hidden, tall), BF16),
@@ -504,13 +672,14 @@
             pltpu.VMEM((enc, hidden), BF16),
             pltpu.VMEM((hidden, hidden), BF16),
             pltpu.VMEM((16, hidden), F32),
-            pltpu.SemaphoreType.DMA((2,)),
+            pltpu.SemaphoreType.DMA((11,)),
             pltpu.SemaphoreType.DMA((9,)),
             pltpu.SemaphoreType.DMA((9,)),
+            pltpu.SemaphoreType.DMA((2, levels_z)),
             pltpu.SemaphoreType.DMA((3,)),
         ],
         compiler_params=pltpu.CompilerParams(
-            collective_id=0, has_side_effects=True, vmem_limit_bytes=48 * 1024 * 1024
+            collective_id=0, has_side_effects=True, vmem_limit_bytes=VMEM_BYTES
         ),
         cost_estimate=pl.CostEstimate(flops=flops, bytes_accessed=1 << 21, transcendentals=slots * hidden * 2),
     )(
@@ -526,13 +695,21 @@
         w3,
         b3,
     )
-    return (
-        g1.astype(F32),
-        gs[:, 0, :],
-        g2.astype(F32),
-        gs[:, 1, :],
-        gs[:, 4:8, :],
-        gs[:, 8:12, 0],
+    shapes = [g1.shape, b1.shape, g2.shape, b2.shape, w3.shape, b3.shape]
+    return tuple(
+        pl.pallas_call(
+            finish,
+            out_shape=[jax.ShapeDtypeStruct(shape, F32) for shape in shapes],
+            in_specs=[hbm] * 3,
+            out_specs=[hbm] * 6,
+            scratch_shapes=[pltpu.VMEM(piece.shape, piece.dtype) for piece in (g1, g2, gs)]
+            + [pltpu.VMEM(shape, F32) for shape in shapes]
+            + [
+                pltpu.SemaphoreType.DMA((2 * blocks + 1,)),
+                pltpu.SemaphoreType.DMA((2 * blocks + 4,)),
+            ],
+            compiler_params=pltpu.CompilerParams(vmem_limit_bytes=VMEM_BYTES),
+        )(g1, g2, gs)
     )
 
 

time: 90.2 us -> 73 us (0.81)
  local copies, waits for them, and re-layouts: 9.5 us -> 0 us
  Pallas kernels: 77.7 us -> 72.2 us
  other arithmetic: 1.83 us -> 0 us
    unnamed x23 -> x0, local copies, waits for them, and re-layouts: 8.22 us -> none
    pallas_call x1, Pallas kernels: 77.7 us -> 70 us  [local(): pl.pallas_call(functools.partial(kernel, (copies, group, levels_z, rays,...]
    pallas_call x0 -> x1, Pallas kernels: none -> 2.23 us  [local(): pl.pallas_call(finish, out_shape=[jax.ShapeDtypeStruct(shape, F32) for sh...]
    convert_element_type x2 -> x0, other arithmetic: 1.83 us -> none  [the longest x1 1.06 us: local(): g2.astype(F32)]
    slice x3 -> x0, local copies, waits for them, and re-layouts: 1.28 us -> none  [the longest x1 0.66 us: local(): gs[:, 8:12, 0]]
where the time goes in v2:
time: 73 us; the launch traced here: 72.8 us
  Pallas kernels  72.2 us (99%)
    pallas_call x1, Pallas kernels, local(): pl.pallas_call(functools.partial(kernel, (copies, group, levels_z, rays,...  70 us
    pallas_call x1, Pallas kernels, local(): pl.pallas_call(finish, out_shape=[jax.ShapeDtypeStruct(shape, F32) for sh...  2.23 us

profile of v2, /device:TPU:1, one launch (start us, length us, event | category | flops | bytes accessed | tf_op | source)
XLA Modules:
  0.0 72.8 jit_solution(16669573400844643904)
XLA Ops:
  0.6 70.0 %shard_map.154 = (bf16[4,96,256]{2,1,0:T(8,128)(2,1)}, bf16[4,256,256]{2,1,0:T(8,128)(2,1)}, f32[4,16,256]{2,1,0:T(8,128)}) custom-call(s32[32,64]{1,0:T(8,128)} %bitcast.2, f32[3,32,64]{2,1,0:T(8,128)} %positions_hbm.1, f32[32,64]{1,0:T(8,128)} %spacing_hbm.1, s32[1,32]{1,0:T(1,128)} %bitcast.3, f32[3,32]{1,0:T(4,128)} %color_grad_hbm.1, ...), custom_call_target="tpu_custom_call" | custom-call | flops 2214592512 | bytes 2097152 | tf_op jit(solution)/shard_map/pallas_call | solution.py:622
  70.6 2.2 %shard_map.155 = (f32[4,96,256]{2,1,0:T(8,128)}, f32[4,256]{1,0:T(4,128)}, f32[4,256,256]{2,1,0:T(8,128)}, f32[4,256]{1,0:T(4,128)}, f32[4,4,256]{2,1,0:T(4,128)}, /*index=5*/f32[4,4]{1,0:T(4,128)}) custom-call(bf16[4,96,256]{2,1,0:T(8,128)(2,1)} %get-tuple-element.9.g1, bf16[4,256,256]{2,1,0:T(8,128)(2,1)} %get-tuple-element.10.g2, ...), custom_call_target="tpu_custom_call" | custom-call | tf_op jit(solution)/shard_map/pallas_call | solution.py:700

commit v3 on v2

--- a/solution.py
+++ b/solution.py
@@ -132,6 +132,8 @@
     send_sem,
     recv_sem,
     near_sem,
+    ring_sem,
+    all_in_sem,
     own_sem,
 ):
     copies, group, levels_z, rays, samples = sizes
@@ -156,26 +158,6 @@
 
     def device_b(peer):
         return {"grp": y, "cell": peer * inner + inside}
-
-    barrier = pltpu.get_barrier_semaphore()
-
-    def greet_a(k, carry):
-        pl.semaphore_signal(
-            barrier, inc=1, device_id=device_a((me + k) % group), device_id_type=MESH
-        )
-        return carry
-
-    def far_first(k):
-        left = levels_z - k
-        odd = left % 2
-        return (z + odd * ((left + 1) // 2) + (1 - odd) * (levels_z - left // 2)) % levels_z
-
-    def greet_b(k, carry):
-        pl.semaphore_signal(barrier, inc=1, device_id=device_b(far_first(k)), device_id_type=MESH)
-        return carry
-
-    lax.fori_loop(1, levels_z, greet_b, 0)
-    lax.fori_loop(1, group, greet_a, 0)
 
     loads = [
         pltpu.make_async_copy(source, target, load_sem.at[i])
@@ -195,7 +177,31 @@
             )
         )
     ]
-    for load in loads:
+    loads[0].start()
+    loads[1].start()
+
+    barrier = pltpu.get_barrier_semaphore()
+    reach = max(1, levels_z // 4)
+
+    def greet_a(k, carry):
+        pl.semaphore_signal(
+            barrier, inc=1, device_id=device_a((me + k) % group), device_id_type=MESH
+        )
+        return carry
+
+    def far_first(k):
+        left = levels_z - k
+        odd = left % 2
+        return (z + odd * ((left + 1) // 2) + (1 - odd) * (levels_z - left // 2)) % levels_z
+
+    def greet_b(k, carry):
+        for peer in ((z + reach + 1 - k) % levels_z, (z + levels_z - reach - 1 + k) % levels_z):
+            pl.semaphore_signal(barrier, inc=1, device_id=device_b(peer), device_id_type=MESH)
+        return carry
+
+    lax.fori_loop(1, reach + 1, greet_b, 0)
+    lax.fori_loop(1, group, greet_a, 0)
+    for load in loads[2:]:
         load.start()
     loads[0].wait()
 
@@ -213,7 +219,7 @@
         others = buffer.at[pl.ds(0, count - 1)]
         pltpu.make_async_copy(others, others, sem).wait()
 
-    def exchange_a(source, target, index):
+    def send_a(source, target, index):
         target[me] = source[me]
 
         def step(k, carry):
@@ -222,6 +228,8 @@
             return carry
 
         lax.fori_loop(1, group, step, 0)
+
+    def wait_a(target, index):
         wait_all(target, group, recv_sem.at[index])
 
     def send_b(source, target, index, row):
@@ -320,6 +328,11 @@
     positions = [pair(positions_ref[k]) for k in range(3)]
     put_a(asend1, spread(positions + [jnp.zeros((rows, lanes), F32)], 3))
 
+    pl.semaphore_wait(barrier, group - 1 + 2 * reach)
+    for peer in ((z + reach) % levels_z, (z + levels_z - reach) % levels_z):
+        pl.semaphore_signal(all_in_sem, inc=1, device_id=device_b(peer), device_id_type=MESH)
+    send_a(asend1, arecv1, 0)
+
     for load in loads[2:]:
         load.wait()
     tall = feat.shape[0]
@@ -343,9 +356,9 @@
     second_sum[...] = jnp.zeros(second_sum.shape, F32)
     og_sum[...] = jnp.zeros(og_sum.shape, F32)
 
-    pl.semaphore_wait(barrier, group - 1 + levels_z - 1)
-    exchange_a(asend1, arecv1, 0)
+    wait_a(arecv1, 0)
     a_to_b(arecv1, bsend1)
+    pl.semaphore_wait(all_in_sem, 2)
     send_b(bsend1, brecv1, 1, 0)
 
     lane_tile = height
@@ -353,78 +366,96 @@
     half_turns = jnp.left_shift(1, level // 2).astype(F32) * jnp.where(
         level % 2 == 1, 0.5 * math.sqrt(2.0), 0.5
     )
-    step_lanes = 4 * lane_tile
-
-    def sources(i):
-        return (z + levels_z - i) % levels_z, (z + i + 1) % levels_z
-
-    def arrivals(target, row, i):
-        first, second = sources(i)
-
-        @pl.when(i > 0)
-        def _():
-            arrival(target, row, first)
-
-        arrival(target, row, second)
-        return first, second
-
-    def encode(point, start):
-        for h in range(2):
-            at = pl.ds(pl.multiple_of(start + h * lane_tile, lane_tile), lane_tile)
-            tall_point = jnp.concatenate(
+    source_lanes = 2 * lane_tile
+    pairs = levels_z // 2 - 1
+    own_start, far_start = 2 * pairs * source_lanes, (2 * pairs + 1) * source_lanes
+    far = (z + levels_z // 2) % levels_z
+
+    def pair_at(d):
+        return ((z + d) % levels_z, (z + levels_z - d) % levels_z), 2 * source_lanes * (d - 1)
+
+    def window(start, count):
+        if not isinstance(start, int):
+            start = pl.multiple_of(start, source_lanes)
+        return pl.ds(start, count * source_lanes)
+
+    def encode(tiles):
+        tall_point = jnp.concatenate(
+            [
+                jnp.concatenate(
+                    [
+                        jnp.broadcast_to(
+                            tile[h * CHANNELS + k : h * CHANNELS + k + 1], (LEVELS, lane_tile)
+                        )
+                        for k in range(3)
+                    ],
+                    axis=0,
+                )
+                for tile in tiles
+                for h in range(2)
+            ],
+            axis=1,
+        )
+        turns = tall_point * jnp.concatenate([half_turns] * (2 * len(tiles)), axis=1)
+        return jnp.concatenate([turns_cosine(turns - 0.25), turns_cosine(turns)], axis=0).astype(
+            BF16
+        )
+
+    def activate(half, act, slope, at):
+        slope[:, at] = half
+        active = (half + half * jnp.tanh(half)).astype(BF16)
+        act[0:hidden, at] = active
+        return active
+
+    def forward(peers, start):
+        at = window(start, len(peers))
+        feat[0:enc, at] = encode([brecv1[peer] for peer in peers])
+        first = activate(matmul(w1t[...], feat[:, at]), act1, slope1, at)
+        bias = jnp.concatenate([b2_wide[...]] * (len(peers) * source_lanes // lanes), axis=1)
+        second = activate(matmul(w2t[...], first) + bias, act2, slope2, at)
+        out = matmul(w3_rows, second)[0:CHANNELS] + b3
+        for s, peer in enumerate(peers):
+            base = s * source_lanes
+            bsend2[peer] = jnp.concatenate(
                 [
-                    jnp.broadcast_to(
-                        point[h * CHANNELS + k : h * CHANNELS + k + 1], (LEVELS, lane_tile)
-                    )
-                    for k in range(3)
+                    out[:, base : base + lane_tile],
+                    out[:, base + lane_tile : base + source_lanes],
                 ],
                 axis=0,
             )
-            turns = tall_point * half_turns
-            feat[0 : 3 * LEVELS, at] = turns_cosine(turns - 0.25).astype(BF16)
-            feat[3 * LEVELS : 6 * LEVELS, at] = turns_cosine(turns).astype(BF16)
-
-    def activate(half, act, slope, at):
-        bent = jnp.tanh(half)
-        product = half * bent
-        active = (half + product).astype(BF16)
-        act[0:hidden, at] = active
-        slope[:, at] = ((half + 1.0) - product) * (0.5 * bent + 0.5)
-        return active
-
-    def forward_step(i, carry):
-        start = i * step_lanes
-        at = pl.ds(pl.multiple_of(start, step_lanes), step_lanes)
-        pair_of = arrivals(brecv1, 0, i)
-        for s, source in enumerate(pair_of):
-            encode(brecv1[source], start + 2 * s * lane_tile)
-        first = activate(matmul(w1t[...], feat[:, at]), act1, slope1, at)
-        bias = jnp.concatenate([b2_wide[...]] * (step_lanes // lanes), axis=1)
-        second = activate(matmul(w2t[...], first) + bias, act2, slope2, at)
-        out = matmul(w3_rows, second)[0:CHANNELS] + b3
-        for s, source in enumerate(pair_of):
-            base = 2 * s * lane_tile
-            bsend2[source] = jnp.concatenate(
-                [
-                    out[:, base : base + lane_tile],
-                    out[:, base + lane_tile : base + 2 * lane_tile],
-                ],
-                axis=0,
-            )
-
-        @pl.when(i > 0)
-        def _():
-            send(bsend2, brecv2, 2, z, pair_of[0], device_b(pair_of[0]), recv_sem.at[2])
-
-        send(bsend2, brecv2, 2, z, pair_of[1], device_b(pair_of[1]), recv_sem.at[2])
+
+    def forward_remote(peers, start):
+        for peer in peers:
+            arrival(brecv1, 0, peer)
+        forward(peers, start)
+        for peer in peers:
+            send(bsend2, brecv2, 2, z, peer, device_b(peer), recv_sem.at[2])
+
+    def forward_pair(d, carry):
+        forward_remote(*pair_at(d))
         return carry
 
-    lax.fori_loop(0, levels_z // 2, forward_step, 0)
+    forward([z], own_start)
+    lax.fori_loop(1, pairs, forward_pair, 0)
+    forward_remote([far], far_start)
+    if pairs > 0:
+        forward_remote(*pair_at(pairs))
+
+    def slope_step(i, carry):
+        at = window(i * source_lanes, 1)
+        for slope in (slope1, slope2):
+            half = slope[:, at]
+            bent = jnp.tanh(half)
+            slope[:, at] = ((half + 1.0) - half * bent) * (0.5 * bent + 0.5)
+        return carry
+
+    lax.fori_loop(0, levels_z, slope_step, 0)
 
     brecv2[z] = bsend2[z]
     wait_all(brecv2, levels_z, recv_sem.at[2])
     b_to_a(brecv2, asend2)
-    exchange_a(asend2, arecv2, 3)
+    send_a(asend2, arecv2, 3)
+    wait_a(arecv2, 3)
     returned = jnp.concatenate(split(get_a(arecv2), 2), axis=1).astype(BF16)
     for g in range(rows):
         at = slice(g * lanes, (g + 1) * lanes)
@@ -474,49 +505,87 @@
         out_grad.append(weight * tint[c] * shade[c] * (1.0 - shade[c]))
 
     put_a(asend3, spread(out_grad, 2))
-    exchange_a(asend3, arecv3, 4)
+    send_a(asend3, arecv3, 4)
+    wait_a(arecv3, 4)
     a_to_b(arecv3, bsend3)
     send_b(bsend3, brecv3, 5, 1)
 
-    def backward_second(i, carry):
-        start = i * step_lanes
-        at = pl.ds(pl.multiple_of(start, step_lanes), step_lanes)
-        pair_of = arrivals(brecv3, 1, i)
-        tiles = [brecv3[source] for source in pair_of]
-        og_sum[...] = og_sum[...] + (tiles[0] + tiles[1])
+    def backward_second(peers, start):
+        at = window(start, len(peers))
+        tiles = [brecv3[peer] for peer in peers]
+        for tile in tiles:
+            og_sum[...] = og_sum[...] + tile
         grad = jnp.concatenate(
             [tile[h * CHANNELS : (h + 1) * CHANNELS] for tile in tiles for h in range(2)], axis=1
         )
         pieces = jnp.concatenate(
-            split(grad, 2) + [jnp.zeros((2 * CHANNELS, step_lanes), F32)], axis=0
+            split(grad, 2) + [jnp.zeros((2 * CHANNELS, grad.shape[1]), F32)], axis=0
         ).astype(BF16)
         og16[:, at] = pieces
         delta = (matmul(w3t[...], pieces) * slope2[:, at]).astype(BF16)
         delta2[:, at] = delta
         second_sum[...] = second_sum[...] + matmul(act1[:, at], delta, NT)
+
+    def backward_pair(d, carry):
+        peers, start = pair_at(d)
+        for peer in peers:
+            arrival(brecv3, 1, peer)
+        backward_second(peers, start)
         return carry
 
-    lax.fori_loop(0, levels_z // 2, backward_second, 0)
+    backward_second([z], own_start)
+    lax.fori_loop(1, pairs + 1, backward_pair, 0)
+    arrival(brecv3, 1, far)
+    backward_second([far], far_start)
     second = second_sum[...]
     g2_own[...] = second[0:hidden].astype(BF16)
 
+    above, below, across = [(y + k) % copies for k in (1, copies - 1, 2)]
+
+    def at_half(ref, part):
+        size = ref.shape[0] // 2
+        return ref.at[pl.ds(part * size, size)]
+
+    def move(source, target, index, arrived, peer):
+        pltpu.make_async_remote_copy(
+            src_ref=source,
+            dst_ref=target,
+            send_sem=send_sem.at[6 + index],
+            recv_sem=arrived,
+            device_id={"grp": peer, "cell": cell},
+            device_id_type=MESH,
+        ).start()
+
     def share(own, out, index):
         pltpu.make_async_copy(own, out.at[y], own_sem.at[index]).start()
-
-        def send(k, carry):
-            pltpu.make_async_remote_copy(
-                src_ref=own,
-                dst_ref=out.at[y],
-                send_sem=send_sem.at[6 + index],
-                recv_sem=recv_sem.at[6 + index],
-                device_id={"grp": (y + k) % copies, "cell": cell},
-                device_id_type=MESH,
-            ).start()
-            return carry
-
-        lax.fori_loop(1, copies, send, 0)
+        for up, down in ((0, 1), (1, 0)):
+            up_half, down_half = at_half(own, up), at_half(own, down)
+            move(up_half, at_half(out.at[y], up), index, ring_sem.at[index, up], above)
+            move(down_half, at_half(out.at[y], down), index, ring_sem.at[index, 2 + down], below)
+
+    def landed(out, index, slot, part, block):
+        half_ref = at_half(out.at[block], part)
+        pltpu.make_async_copy(half_ref, half_ref, ring_sem.at[index, slot]).wait()
+
+    def pass_on(out, index):
+        landed(out, index, 0, 0, below)
+        half_ref = at_half(out.at[below], 0)
+        move(half_ref, half_ref, index, ring_sem.at[index, 4], above)
+        landed(out, index, 3, 1, above)
+        half_ref = at_half(out.at[above], 1)
+        move(half_ref, half_ref, index, ring_sem.at[index, 5], below)
+
+    def gathered(own, out, index):
+        pltpu.make_async_copy(own, out.at[y], own_sem.at[index]).wait()
+        landed(out, index, 1, 1, below)
+        landed(out, index, 2, 0, above)
+        landed(out, index, 4, 0, across)
+        landed(out, index, 5, 1, across)
+        wait_all(out, copies, send_sem.at[6 + index])
 
     share(g2_own, g2_out, 0)
+
+    step_lanes = 2 * source_lanes
 
     def backward_first(i, carry):
         at = pl.ds(pl.multiple_of(i * step_lanes, step_lanes), step_lanes)
@@ -527,6 +596,7 @@
     first = matmul(feat[...], delta1[...], NT)
     g1_own[...] = first[0:enc].astype(BF16)
     share(g1_own, g1_out, 1)
+    pass_on(g2_out, 0)
     third = matmul(og16[...], act2[...], NT)
     og_total = jnp.sum(og_sum[...], axis=1, keepdims=True)
     og_total = og_total[0:CHANNELS] + og_total[CHANNELS : 2 * CHANNELS]
@@ -549,12 +619,16 @@
         ],
         axis=0,
     )
-    share(gs_own, gs_out, 2)
-
-    for own, out, index in ((g2_own, g2_out, 0), (g1_own, g1_out, 1), (gs_own, gs_out, 2)):
-        pltpu.make_async_copy(own, out.at[y], own_sem.at[index]).wait()
-        wait_all(out, copies, recv_sem.at[6 + index])
-        wait_all(out, copies, send_sem.at[6 + index])
+    pltpu.make_async_copy(gs_own, gs_out.at[y], own_sem.at[2]).start()
+    for peer in (across, above, below):
+        move(gs_own, gs_out.at[y], 2, recv_sem.at[8], peer)
+    pass_on(g1_out, 1)
+
+    gathered(g2_own, g2_out, 0)
+    gathered(g1_own, g1_out, 1)
+    pltpu.make_async_copy(gs_own, gs_out.at[y], own_sem.at[2]).wait()
+    wait_all(gs_out, copies, recv_sem.at[8])
+    wait_all(gs_out, copies, send_sem.at[8])
     wait_all(asend1, group, send_sem.at[0])
     wait_all(bsend1, levels_z, send_sem.at[1])
     wait_all(bsend2, levels_z, send_sem.at[2])
@@ -676,6 +750,8 @@
             pltpu.SemaphoreType.DMA((9,)),
             pltpu.SemaphoreType.DMA((9,)),
             pltpu.SemaphoreType.DMA((2, levels_z)),
+            pltpu.SemaphoreType.DMA((2, 6)),
+            pltpu.SemaphoreType.REGULAR,
             pltpu.SemaphoreType.DMA((3,)),
         ],
         compiler_params=pltpu.CompilerParams(

time: 73 us -> 69.3 us (0.949)
  Pallas kernels: 72.2 us -> 67.9 us
    pallas_call x1, Pallas kernels: 70 us -> 65.7 us  [local(): pl.pallas_call(functools.partial(kernel, (copies, group, levels_z, rays,...]
where the time goes in v3:
time: 69.3 us; the launch traced here: 68.6 us
  Pallas kernels  67.9 us (98%)
    pallas_call x1, Pallas kernels, local(): pl.pallas_call(functools.partial(kernel, (copies, group, levels_z, rays,...  65.7 us
    pallas_call x1, Pallas kernels, local(): pl.pallas_call(finish, out_shape=[jax.ShapeDtypeStruct(shape, F32) for sh...  2.23 us

profile of v3, /device:TPU:1, one launch (start us, length us, event | category | flops | bytes accessed | tf_op | source)
XLA Modules:
  0.0 68.6 jit_solution(834248268632731099)
XLA Ops:
  0.6 65.7 %shard_map.154 = (bf16[4,96,256]{2,1,0:T(8,128)(2,1)}, bf16[4,256,256]{2,1,0:T(8,128)(2,1)}, f32[4,16,256]{2,1,0:T(8,128)}) custom-call(s32[32,64]{1,0:T(8,128)} %bitcast.2, f32[3,32,64]{2,1,0:T(8,128)} %positions_hbm.1, f32[32,64]{1,0:T(8,128)} %spacing_hbm.1, s32[1,32]{1,0:T(1,128)} %bitcast.3, f32[3,32]{1,0:T(4,128)} %color_grad_hbm.1, ...), custom_call_target="tpu_custom_call" | custom-call | flops 2214592512 | bytes 2097152 | tf_op jit(solution)/shard_map/pallas_call | solution.py:696
  66.4 2.2 %shard_map.155 = (f32[4,96,256]{2,1,0:T(8,128)}, f32[4,256]{1,0:T(4,128)}, f32[4,256,256]{2,1,0:T(8,128)}, f32[4,256]{1,0:T(4,128)}, f32[4,4,256]{2,1,0:T(4,128)}, /*index=5*/f32[4,4]{1,0:T(4,128)}) custom-call(bf16[4,96,256]{2,1,0:T(8,128)(2,1)} %get-tuple-element.9.g1, bf16[4,256,256]{2,1,0:T(8,128)(2,1)} %get-tuple-element.10.g2, ...), custom_call_target="tpu_custom_call" | custom-call | tf_op jit(solution)/shard_map/pallas_call | solution.py:776

commit v4 on v3

--- a/solution.py
+++ b/solution.py
@@ -58,15 +58,13 @@
     lanes = tiles.shape[2]
     part = lanes // 8
     sub = lax.broadcasted_iota(jnp.int32, tiles.shape, 1)
-    lane = lax.broadcasted_iota(jnp.int32, tiles.shape, 2) // part
-    for bit in (1, 2, 4):
-        low = pltpu.roll(pltpu.roll(tiles, 8 - bit, 1), bit * part, 2)
-        high = pltpu.roll(pltpu.roll(tiles, bit, 1), lanes - bit * part, 2)
-        sub_set = (sub & bit) != 0
-        lane_set = (lane & bit) != 0
-        moved = jnp.where(lane_set, low, high)
-        tiles = jnp.where(sub_set == lane_set, tiles, moved)
-    return tiles
+    eighth = lax.broadcasted_iota(jnp.int32, tiles.shape, 2) // part
+    apart = (eighth - sub) & 7
+    result = tiles
+    for d in range(1, 8):
+        moved = pltpu.roll(pltpu.roll(tiles, 8 - d, 1), d * part, 2)
+        result = jnp.where(apart == d, moved, result)
+    return result
 
 
 def kernel(
@@ -149,12 +147,30 @@
 
     y = lax.axis_index("grp")
     cell = lax.axis_index("cell")
-    z = cell // inner
-    inside = cell % inner
+    z = lax.div(cell, jnp.int32(inner))
+    inside = cell - z * inner
     me = y * inner + inside
-
-    def device_a(peer):
-        return {"grp": peer // inner, "cell": z * inner + peer % inner}
+    cores = 2 if inner % 2 == 0 else 1
+    ring_x = inner // cores
+    x = lax.div(inside, jnp.int32(cores))
+    core = inside - x * cores
+
+    def around(place, count):
+        return [place] + [lax.rem(place + d, jnp.int32(count)) for d in range(1, count)]
+
+    def hops(d, count):
+        return min(d, count - d)
+
+    on_y, on_x, on_core = around(y, copies), around(x, ring_x), around(core, cores)
+    on_z = around(z, levels_z)
+    steps_a = sorted(
+        ((dy, dx, dc) for dy in range(copies) for dx in range(ring_x) for dc in range(cores)),
+        key=lambda d: -hops(d[0], copies) - hops(d[1], ring_x),
+    )
+    peers_a = [
+        (on_y[dy], on_x[dx] * cores + on_core[dc]) for dy, dx, dc in steps_a if dy or dx or dc
+    ]
+    steps_b = sorted(range(1, levels_z), key=lambda d: -hops(d, levels_z))
 
     def device_b(peer):
         return {"grp": y, "cell": peer * inner + inside}
@@ -182,25 +198,16 @@
 
     barrier = pltpu.get_barrier_semaphore()
     reach = max(1, levels_z // 4)
-
-    def greet_a(k, carry):
+    near_b = [d for d in steps_b if hops(d, levels_z) <= reach]
+    for d in near_b:
+        pl.semaphore_signal(barrier, inc=1, device_id=device_b(on_z[d]), device_id_type=MESH)
+    for peer_y, peer_in in peers_a:
         pl.semaphore_signal(
-            barrier, inc=1, device_id=device_a((me + k) % group), device_id_type=MESH
+            barrier,
+            inc=1,
+            device_id={"grp": peer_y, "cell": z * inner + peer_in},
+            device_id_type=MESH,
         )
-        return carry
-
-    def far_first(k):
-        left = levels_z - k
-        odd = left % 2
-        return (z + odd * ((left + 1) // 2) + (1 - odd) * (levels_z - left // 2)) % levels_z
-
-    def greet_b(k, carry):
-        for peer in ((z + reach + 1 - k) % levels_z, (z + levels_z - reach - 1 + k) % levels_z):
-            pl.semaphore_signal(barrier, inc=1, device_id=device_b(peer), device_id_type=MESH)
-        return carry
-
-    lax.fori_loop(1, reach + 1, greet_b, 0)
-    lax.fori_loop(1, group, greet_a, 0)
     for load in loads[2:]:
         load.start()
     loads[0].wait()
@@ -222,12 +229,9 @@
     def send_a(source, target, index):
         target[me] = source[me]
 
-        def step(k, carry):
-            peer = (me + k) % group
-            send(source, target, index, me, peer, device_a(peer), recv_sem.at[index])
-            return carry
-
-        lax.fori_loop(1, group, step, 0)
+        for peer_y, peer_in in peers_a:
+            device = {"grp": peer_y, "cell": z * inner + peer_in}
+            send(source, target, index, me, peer_y * inner + peer_in, device, recv_sem.at[index])
 
     def wait_a(target, index):
         wait_all(target, group, recv_sem.at[index])
@@ -235,12 +239,8 @@
     def send_b(source, target, index, row):
         target[z] = source[z]
 
-        def step(k, carry):
-            peer = far_first(k)
-            send(source, target, index, z, peer, device_b(peer), near_sem.at[row, z])
-            return carry
-
-        lax.fori_loop(1, levels_z, step, 0)
+        for d in steps_b:
+            send(source, target, index, z, on_z[d], device_b(on_z[d]), near_sem.at[row, z])
 
     def arrival(target, row, peer):
         pltpu.make_async_copy(target.at[peer], target.at[peer], near_sem.at[row, peer]).wait()
@@ -328,9 +328,9 @@
     positions = [pair(positions_ref[k]) for k in range(3)]
     put_a(asend1, spread(positions + [jnp.zeros((rows, lanes), F32)], 3))
 
-    pl.semaphore_wait(barrier, group - 1 + 2 * reach)
-    for peer in ((z + reach) % levels_z, (z + levels_z - reach) % levels_z):
-        pl.semaphore_signal(all_in_sem, inc=1, device_id=device_b(peer), device_id_type=MESH)
+    pl.semaphore_wait(barrier, group - 1 + len(near_b))
+    for d in (reach, levels_z - reach):
+        pl.semaphore_signal(all_in_sem, inc=1, device_id=device_b(on_z[d]), device_id_type=MESH)
     send_a(asend1, arecv1, 0)
 
     for load in loads[2:]:
@@ -353,7 +353,6 @@
     feat[enc:tall, :] = jnp.where(one_row, 1.0, 0.0).astype(BF16)
     act1[hidden:, :] = jnp.ones((act1.shape[0] - hidden, slots), BF16)
 
-    second_sum[...] = jnp.zeros(second_sum.shape, F32)
     og_sum[...] = jnp.zeros(og_sum.shape, F32)
 
     wait_a(arecv1, 0)
@@ -369,10 +368,11 @@
     source_lanes = 2 * lane_tile
     pairs = levels_z // 2 - 1
     own_start, far_start = 2 * pairs * source_lanes, (2 * pairs + 1) * source_lanes
-    far = (z + levels_z // 2) % levels_z
+    far = on_z[levels_z // 2]
 
     def pair_at(d):
-        return ((z + d) % levels_z, (z + levels_z - d) % levels_z), 2 * source_lanes * (d - 1)
+        ring = jnp.int32(levels_z)
+        return (lax.rem(z + d, ring), lax.rem(z + levels_z - d, ring)), 2 * source_lanes * (d - 1)
 
     def window(start, count):
         if not isinstance(start, int):
@@ -451,6 +451,29 @@
 
     lax.fori_loop(0, levels_z, slope_step, 0)
 
+    lane = lax.broadcasted_iota(jnp.int32, (rows, lanes), 1)
+    left = lane < samples
+
+    def per_ray(row):
+        tall_row = column(row)
+        return jnp.where(left, tall_row[:rows], tall_row[rows:])
+
+    lengths = per_ray(lengths_ref[...].astype(F32))
+    tint = [per_ray(color_grad_ref[c : c + 1, :]) for c in range(3)]
+    spacing = pair(spacing_ref[...])
+    before = lax.broadcasted_iota(jnp.int32, (lanes, lanes), 0)
+    after = lax.broadcasted_iota(jnp.int32, (lanes, lanes), 1)
+    same_ray = (before // samples) == (after // samples)
+
+    earlier_mask = jnp.where((before < after) & same_ray, 1.0, 0.0).astype(BF16)
+    later_mask = jnp.where((before > after) & same_ray, 1.0, 0.0).astype(BF16)
+
+    def scan(values, mask):
+        pieces = jnp.concatenate(split(values, 3), axis=0).astype(BF16)
+        sums = matmul(pieces, mask)
+        return sums[0:rows] + sums[rows : 2 * rows] + sums[2 * rows : 3 * rows]
+
+    live = (lane % samples).astype(F32) < lengths
     brecv2[z] = bsend2[z]
     wait_all(brecv2, levels_z, recv_sem.at[2])
     b_to_a(brecv2, asend2)
@@ -465,27 +488,6 @@
         v8[g] = both
     field = [v8[:, c, :] + v8[:, c + CHANNELS, :] for c in range(CHANNELS)]
 
-    lane = lax.broadcasted_iota(jnp.int32, (rows, lanes), 1)
-    left = lane < samples
-
-    def per_ray(row):
-        tall_row = column(row)
-        return jnp.where(left, tall_row[:rows], tall_row[rows:])
-
-    lengths = per_ray(lengths_ref[...].astype(F32))
-    tint = [per_ray(color_grad_ref[c : c + 1, :]) for c in range(3)]
-    spacing = pair(spacing_ref[...])
-    before = lax.broadcasted_iota(jnp.int32, (lanes, lanes), 0)
-    after = lax.broadcasted_iota(jnp.int32, (lanes, lanes), 1)
-    same_ray = (before // samples) == (after // samples)
-
-    def scan(values, mask):
-        ones = jnp.where(mask & same_ray, 1.0, 0.0).astype(BF16)
-        pieces = jnp.concatenate(split(values, 3), axis=0).astype(BF16)
-        sums = matmul(pieces, ones)
-        return sums[0:rows] + sums[rows : 2 * rows] + sums[2 * rows : 3 * rows]
-
-    live = (lane % samples).astype(F32) < lengths
     density = jnp.maximum(field[0], 0.0) + jnp.log1p(jnp.exp(-jnp.abs(field[0])))
     step = jnp.where(live, density * spacing, 0.0)
     left_over = jnp.exp(-step)
@@ -493,11 +495,11 @@
         1.0 - step * (1 / 2) * (1.0 - step * (1 / 3) * (1.0 - step * (1 / 4) * (1.0 - step * (1 / 5))))
     )
     absorbed = jnp.where(step < 0.05, series, 1.0 - left_over)
-    trans = jnp.exp(-scan(step, before < after))
+    trans = jnp.exp(-scan(step, earlier_mask))
     weight = trans * absorbed
     shade = [0.5 + 0.5 * jnp.tanh(0.5 * field[c]) for c in range(1, CHANNELS)]
     seen = tint[0] * shade[0] + tint[1] * shade[1] + tint[2] * shade[2]
-    behind = scan(weight * seen, before > after)
+    behind = scan(weight * seen, later_mask)
     step_grad = trans * left_over * seen - behind
     density_slope = 0.5 + 0.5 * jnp.tanh(0.5 * field[0])
     out_grad = [jnp.where(live, step_grad * spacing * density_slope, 0.0)]
@@ -524,23 +526,22 @@
         og16[:, at] = pieces
         delta = (matmul(w3t[...], pieces) * slope2[:, at]).astype(BF16)
         delta2[:, at] = delta
-        second_sum[...] = second_sum[...] + matmul(act1[:, at], delta, NT)
+        return matmul(act1[:, at], delta, NT)
 
     def backward_pair(d, carry):
         peers, start = pair_at(d)
         for peer in peers:
             arrival(brecv3, 1, peer)
-        backward_second(peers, start)
+        second_sum[...] = second_sum[...] + backward_second(peers, start)
         return carry
 
-    backward_second([z], own_start)
+    second_sum[...] = backward_second([z], own_start)
     lax.fori_loop(1, pairs + 1, backward_pair, 0)
     arrival(brecv3, 1, far)
-    backward_second([far], far_start)
-    second = second_sum[...]
+    second = second_sum[...] + backward_second([far], far_start)
     g2_own[...] = second[0:hidden].astype(BF16)
 
-    above, below, across = [(y + k) % copies for k in (1, copies - 1, 2)]
+    above, below, across = on_y[1], on_y[copies - 1], on_y[2]
 
     def at_half(ref, part):
         size = ref.shape[0] // 2

time: 69.3 us -> 68 us (0.981)
  Pallas kernels: 67.9 us -> 66.6 us
    pallas_call x1, Pallas kernels: 65.7 us -> 64.4 us  [local(): pl.pallas_call(functools.partial(kernel, (copies, group, levels_z, rays,...]
where the time goes in v4:
time: 68 us; the launch traced here: 67.3 us
  Pallas kernels  66.6 us (98%)
    pallas_call x1, Pallas kernels, local(): pl.pallas_call(functools.partial(kernel, (copies, group, levels_z, rays,...  64.4 us
    pallas_call x1, Pallas kernels, local(): pl.pallas_call(finish, out_shape=[jax.ShapeDtypeStruct(shape, F32) for sh...  2.23 us

profile of v4, /device:TPU:1, one launch (start us, length us, event | category | flops | bytes accessed | tf_op | source)
XLA Modules:
  0.0 67.3 jit_solution(9509128111430827836)
XLA Ops:
  0.6 64.4 %shard_map.154 = (bf16[4,96,256]{2,1,0:T(8,128)(2,1)}, bf16[4,256,256]{2,1,0:T(8,128)(2,1)}, f32[4,16,256]{2,1,0:T(8,128)}) custom-call(s32[32,64]{1,0:T(8,128)} %bitcast.2, f32[3,32,64]{2,1,0:T(8,128)} %positions_hbm.1, f32[32,64]{1,0:T(8,128)} %spacing_hbm.1, s32[1,32]{1,0:T(1,128)} %bitcast.3, f32[3,32]{1,0:T(4,128)} %color_grad_hbm.1, ...), custom_call_target="tpu_custom_call" | custom-call | flops 2214592512 | bytes 2097152 | tf_op jit(solution)/shard_map/pallas_call | solution.py:697
  65.0 2.2 %shard_map.155 = (f32[4,96,256]{2,1,0:T(8,128)}, f32[4,256]{1,0:T(4,128)}, f32[4,256,256]{2,1,0:T(8,128)}, f32[4,256]{1,0:T(4,128)}, f32[4,4,256]{2,1,0:T(4,128)}, /*index=5*/f32[4,4]{1,0:T(4,128)}) custom-call(bf16[4,96,256]{2,1,0:T(8,128)(2,1)} %get-tuple-element.9.g1, bf16[4,256,256]{2,1,0:T(8,128)(2,1)} %get-tuple-element.10.g2, ...), custom_call_target="tpu_custom_call" | custom-call | tf_op jit(solution)/shard_map/pallas_call | solution.py:777

commit v5 on v4

--- a/solution.py
+++ b/solution.py
@@ -95,6 +95,7 @@
     v8,
     av,
     bt2,
+    bt_turned,
     asend1,
     arecv1,
     bsend1,
@@ -227,20 +228,18 @@
         pltpu.make_async_copy(others, others, sem).wait()
 
     def send_a(source, target, index):
-        target[me] = source[me]
-
         for peer_y, peer_in in peers_a:
             device = {"grp": peer_y, "cell": z * inner + peer_in}
             send(source, target, index, me, peer_y * inner + peer_in, device, recv_sem.at[index])
+        target[me] = source[me]
 
     def wait_a(target, index):
         wait_all(target, group, recv_sem.at[index])
 
     def send_b(source, target, index, row):
-        target[z] = source[z]
-
         for d in steps_b:
             send(source, target, index, z, on_z[d], device_b(on_z[d]), near_sem.at[row, z])
+        target[z] = source[z]
 
     def arrival(target, row, peer):
         pltpu.make_async_copy(target.at[peer], target.at[peer], near_sem.at[row, peer]).wait()
@@ -279,7 +278,7 @@
         bt2[0:width, g * lanes : (g + 1) * lanes] = hit
         bt2[width : 2 * width, g * lanes : (g + 1) * lanes] = hit
 
-    def spread(channels, parts):
+    def spread(channels, parts, turned=False):
         for c in range(CHANNELS):
             values = channels[c]
             v8[:, c, :] = values
@@ -291,7 +290,10 @@
                 av[p * height : (p + 1) * height, g * lanes : (g + 1) * lanes] = jnp.where(
                     mine, tall, 0.0
                 ).astype(BF16)
-        wide = matmul(av[0 : parts * height], bt2[0:width], NT)
+        if turned:
+            wide = matmul(av[0 : parts * height], bt_turned[...])
+        else:
+            wide = matmul(av[0 : parts * height], bt2[0:width], NT)
         result = wide[0:height]
         for p in range(1, parts):
             result = result + wide[p * height : (p + 1) * height]
@@ -354,6 +356,10 @@
     act1[hidden:, :] = jnp.ones((act1.shape[0] - hidden, slots), BF16)
 
     og_sum[...] = jnp.zeros(og_sum.shape, F32)
+
+    for g in range(rows):
+        at = slice(g * lanes, (g + 1) * lanes)
+        bt_turned[at, :] = bt2[0:width, at].astype(F32).T.astype(BF16)
 
     wait_a(arecv1, 0)
     a_to_b(arecv1, bsend1)
@@ -480,12 +486,13 @@
     send_a(asend2, arecv2, 3)
     wait_a(arecv2, 3)
     returned = jnp.concatenate(split(get_a(arecv2), 2), axis=1).astype(BF16)
-    for g in range(rows):
-        at = slice(g * lanes, (g + 1) * lanes)
-        found = matmul(returned, bt2[:, at])
-        kept = jnp.where(owner_row == keys_a[g], found, 0.0)
-        both = jnp.sum(kept.reshape(height // 8, 8, lanes), axis=0)
-        v8[g] = both
+    for g in range(0, rows, 2):
+        found = matmul(returned, bt2[:, g * lanes : (g + 2) * lanes])
+        for k in range(2):
+            kept = jnp.where(
+                owner_row == keys_a[g + k], found[:, k * lanes : (k + 1) * lanes], 0.0
+            )
+            v8[g + k] = jnp.sum(kept.reshape(height // 8, 8, lanes), axis=0)
     field = [v8[:, c, :] + v8[:, c + CHANNELS, :] for c in range(CHANNELS)]
 
     density = jnp.maximum(field[0], 0.0) + jnp.log1p(jnp.exp(-jnp.abs(field[0])))
@@ -506,7 +513,7 @@
     for c in range(3):
         out_grad.append(weight * tint[c] * shade[c] * (1.0 - shade[c]))
 
-    put_a(asend3, spread(out_grad, 2))
+    put_a(asend3, spread(out_grad, 2, turned=True))
     send_a(asend3, arecv3, 4)
     wait_a(arecv3, 4)
     a_to_b(arecv3, bsend3)
@@ -613,10 +620,9 @@
         [
             first[enc : enc + 1],
             second[hidden : hidden + 1],
-            jnp.zeros((2, hidden), F32),
+            third_bias,
+            jnp.zeros((1, hidden), F32),
             third[0:CHANNELS] + third[CHANNELS : 2 * CHANNELS],
-            third_bias,
-            jnp.zeros((7, hidden), F32),
         ],
         axis=0,
     )
@@ -661,7 +667,7 @@
         b1_f[b : b + 1, :] = gs_b[b, 0:1, :]
         b2_f[b : b + 1, :] = gs_b[b, 1:2, :]
         g3_f[b] = gs_b[b, 4:8, :]
-        b3_f[b : b + 1, :] = gs_b[b, 8:9, 0 : b3_f.shape[1]]
+        b3_f[b : b + 1, :] = gs_b[b, 2:3, 0 : b3_f.shape[1]]
     put(b1_f, b1_out)
     put(b2_f, b2_out)
     put(g3_f, g3_out)
@@ -699,7 +705,7 @@
         out_shape=[
             jax.ShapeDtypeStruct((blocks, enc, hidden), BF16),
             jax.ShapeDtypeStruct((blocks, hidden, hidden), BF16),
-            jax.ShapeDtypeStruct((blocks, 16, hidden), F32),
+            jax.ShapeDtypeStruct((blocks, 8, hidden), F32),
         ],
         in_specs=[hbm] * 11,
         out_specs=[hbm] * 3,
@@ -716,6 +722,7 @@
             pltpu.VMEM((rows, 8, lanes), F32),
             pltpu.VMEM((3 * height, total), BF16),
             pltpu.VMEM((2 * width, total), BF16),
+            pltpu.VMEM((total, width), BF16),
             part_a,
             part_a,
             part_b,
@@ -746,7 +753,7 @@
             pltpu.VMEM((hidden, lanes), F32),
             pltpu.VMEM((enc, hidden), BF16),
             pltpu.VMEM((hidden, hidden), BF16),
-            pltpu.VMEM((16, hidden), F32),
+            pltpu.VMEM((8, hidden), F32),
             pltpu.SemaphoreType.DMA((11,)),
             pltpu.SemaphoreType.DMA((9,)),
             pltpu.SemaphoreType.DMA((9,)),

time: 68 us -> 67.6 us (level)
  no operation moved by 1% of the time
where the time goes in v5:
time: 67.6 us; the launch traced here: 67 us
  Pallas kernels  66.3 us (98%)
    pallas_call x1, Pallas kernels, local(): pl.pallas_call(functools.partial(kernel, (copies, group, levels_z, rays,...  64.1 us
    pallas_call x1, Pallas kernels, local(): pl.pallas_call(finish, out_shape=[jax.ShapeDtypeStruct(shape, F32) for sh...  2.21 us

profile of v5, /device:TPU:1, one launch (start us, length us, event | category | flops | bytes accessed | tf_op | source)
XLA Modules:
  0.0 67.0 jit_solution(222783862371527429)
XLA Ops:
  0.6 64.1 %shard_map.154 = (bf16[4,96,256]{2,1,0:T(8,128)(2,1)}, bf16[4,256,256]{2,1,0:T(8,128)(2,1)}, f32[4,8,256]{2,1,0:T(8,128)}) custom-call(s32[32,64]{1,0:T(8,128)} %bitcast.2, f32[3,32,64]{2,1,0:T(8,128)} %positions_hbm.1, f32[32,64]{1,0:T(8,128)} %spacing_hbm.1, s32[1,32]{1,0:T(1,128)} %bitcast.3, f32[3,32]{1,0:T(4,128)} %color_grad_hbm.1, ...), custom_call_target="tpu_custom_call" | custom-call | flops 2214592512 | bytes 2097152 | tf_op jit(solution)/shard_map/pallas_call | solution.py:703
  64.8 2.2 %shard_map.155 = (f32[4,96,256]{2,1,0:T(8,128)}, f32[4,256]{1,0:T(4,128)}, f32[4,256,256]{2,1,0:T(8,128)}, f32[4,256]{1,0:T(4,128)}, f32[4,4,256]{2,1,0:T(4,128)}, /*index=5*/f32[4,4]{1,0:T(4,128)}) custom-call(bf16[4,96,256]{2,1,0:T(8,128)(2,1)} %get-tuple-element.9.g1, bf16[4,256,256]{2,1,0:T(8,128)(2,1)} %get-tuple-element.10.g2, ...), custom_call_target="tpu_custom_call" | custom-call | tf_op jit(solution)/shard_map/pallas_call | solution.py:784

commit v6 on v5

--- a/solution.py
+++ b/solution.py
@@ -115,7 +115,7 @@
     slope2,
     delta1,
     delta2,
-    og16,
+    third_sum,
     og_sum,
     second_sum,
     w1_own,
@@ -356,6 +356,7 @@
     act1[hidden:, :] = jnp.ones((act1.shape[0] - hidden, slots), BF16)
 
     og_sum[...] = jnp.zeros(og_sum.shape, F32)
+    third_sum[...] = jnp.zeros(third_sum.shape, F32)
 
     for g in range(rows):
         at = slice(g * lanes, (g + 1) * lanes)
@@ -443,9 +444,9 @@
 
     forward([z], own_start)
     lax.fori_loop(1, pairs, forward_pair, 0)
-    forward_remote([far], far_start)
     if pairs > 0:
         forward_remote(*pair_at(pairs))
+    forward_remote([far], far_start)
 
     def slope_step(i, carry):
         at = window(i * source_lanes, 1)
@@ -530,9 +531,9 @@
         pieces = jnp.concatenate(
             split(grad, 2) + [jnp.zeros((2 * CHANNELS, grad.shape[1]), F32)], axis=0
         ).astype(BF16)
-        og16[:, at] = pieces
         delta = (matmul(w3t[...], pieces) * slope2[:, at]).astype(BF16)
         delta2[:, at] = delta
+        third_sum[...] = third_sum[...] + matmul(pieces, act2[:, at], NT)
         return matmul(act1[:, at], delta, NT)
 
     def backward_pair(d, carry):
@@ -605,7 +606,7 @@
     g1_own[...] = first[0:enc].astype(BF16)
     share(g1_own, g1_out, 1)
     pass_on(g2_out, 0)
-    third = matmul(og16[...], act2[...], NT)
+    third = third_sum[...]
     og_total = jnp.sum(og_sum[...], axis=1, keepdims=True)
     og_total = og_total[0:CHANNELS] + og_total[CHANNELS : 2 * CHANNELS]
     diagonal = lax.broadcasted_iota(jnp.int32, (CHANNELS, hidden), 0) == lax.broadcasted_iota(
@@ -742,7 +743,7 @@
             pltpu.VMEM((hidden, slots), F32),
             pltpu.VMEM((hidden, slots), BF16),
             pltpu.VMEM((hidden, slots), BF16),
-            pltpu.VMEM((4 * CHANNELS, slots), BF16),
+            pltpu.VMEM((4 * CHANNELS, hidden), F32),
             pltpu.VMEM((8, height), F32),
             pltpu.VMEM((hidden + 16, hidden), F32),
             pltpu.VMEM((enc, hidden), BF16),

time: 67.6 us -> 68.4 us (1.012)
  Pallas kernels: 66.3 us -> 67.6 us
    pallas_call x1, Pallas kernels: 64.1 us -> 65.4 us  [local(): pl.pallas_call(functools.partial(kernel, (copies, group, levels_z, rays,...]
where the time goes in v6:
time: 68.4 us; the launch traced here: 68.2 us
  Pallas kernels  67.6 us (99%)
    pallas_call x1, Pallas kernels, local(): pl.pallas_call(functools.partial(kernel, (copies, group, levels_z, rays,...  65.4 us
    pallas_call x1, Pallas kernels, local(): pl.pallas_call(finish, out_shape=[jax.ShapeDtypeStruct(shape, F32) for sh...  2.21 us

profile of v6, /device:TPU:1, one launch (start us, length us, event | category | flops | bytes accessed | tf_op | source)
XLA Modules:
  0.0 68.2 jit_solution(2541931020217181700)
XLA Ops:
  0.6 65.4 %shard_map.154 = (bf16[4,96,256]{2,1,0:T(8,128)(2,1)}, bf16[4,256,256]{2,1,0:T(8,128)(2,1)}, f32[4,8,256]{2,1,0:T(8,128)}) custom-call(s32[32,64]{1,0:T(8,128)} %bitcast.2, f32[3,32,64]{2,1,0:T(8,128)} %positions_hbm.1, f32[32,64]{1,0:T(8,128)} %spacing_hbm.1, s32[1,32]{1,0:T(1,128)} %bitcast.3, f32[3,32]{1,0:T(4,128)} %color_grad_hbm.1, ...), custom_call_target="tpu_custom_call" | custom-call | flops 2214592512 | bytes 2097152 | tf_op jit(solution)/shard_map/pallas_call | solution.py:704
  66.0 2.2 %shard_map.155 = (f32[4,96,256]{2,1,0:T(8,128)}, f32[4,256]{1,0:T(4,128)}, f32[4,256,256]{2,1,0:T(8,128)}, f32[4,256]{1,0:T(4,128)}, f32[4,4,256]{2,1,0:T(4,128)}, /*index=5*/f32[4,4]{1,0:T(4,128)}) custom-call(bf16[4,96,256]{2,1,0:T(8,128)(2,1)} %get-tuple-element.9.g1, bf16[4,256,256]{2,1,0:T(8,128)(2,1)} %get-tuple-element.10.g2, ...), custom_call_target="tpu_custom_call" | custom-call | tf_op jit(solution)/shard_map/pallas_call | solution.py:785
